TPU v7x, 256 devices: a whole 4x4x8 slice. The times are simulated.
256 devices in a mesh: dp: 64 (over x, z, y_lo), head: 4 (over y_hi, core).
Axes of the slice: x: 4, y: 4 (y_hi: 2, y_lo: 2; y = y_hi * 2 + y_lo), z: 8, core: 2. Of those that a mesh axis runs over, the one named last changes fastest.
Arguments:
- feat_img: bfloat16 [8192, 1280], P('dp'), as said below
- feat_txt: bfloat16 [8192, 1280], P('dp'), as said below
- w_img: bfloat16 [1280, 1024], P(None, 'head'), as said below
- w_txt: bfloat16 [1280, 1024], P(None, 'head'), as said below
- logit_scale: float32 [], replicated, may hold values from 10 to 100
Outputs:
- grad_w_img: float32 [1280, 1024], P('dp', 'head')
- grad_w_txt: float32 [1280, 1024], P('dp', 'head')
Inputs may be any that keep to these rules, and one draw needn't show every extreme that they name: `feat_img`: Real-valued features; rows differ in scale. `feat_txt`: Real-valued features. `w_img`: entries of order 1280 ** -0.5. `w_txt`: entries of order 1280 ** -0.5.
All inputs are finite; a program needn't handle non-finite values.
Results may differ from a plain program's by a relative error of at most 0.0041.
Values may be sent and summed in bfloat16 or wider, within the bound.
A program may use at most 128 MiB of HBM per device.

v0:
```python
import jax
import jax.numpy as jnp
from jax import lax
from jax.sharding import PartitionSpec as P


def merged(array, axis, combine):
    everything = jax.tree.map(lambda part: lax.all_gather(part, axis), array)
    initial = jax.tree.map(lambda part: part[0], everything)

    def step(k, so_far):
        return combine(so_far, jax.tree.map(lambda part: part[k], everything))

    return lax.fori_loop(1, lax.axis_size(axis), step, initial)


def combine_totals(first, second):
    top = jnp.maximum(first[0], second[0])
    return (top, first[1] * jnp.exp(first[0] - top) + second[1] * jnp.exp(second[0] - top))


def per_device(feat_img, feat_txt, w_img, w_txt, logit_scale):
    rows = feat_img.shape[0]
    cols = w_img.shape[1]
    total = rows * lax.axis_size("dp")
    img_raw = jnp.dot(feat_img, w_img, preferred_element_type=jnp.float32)
    txt_raw = jnp.dot(feat_txt, w_txt, preferred_element_type=jnp.float32)
    img_sq, txt_sq = lax.psum(
        (jnp.sum(img_raw * img_raw, axis=1), jnp.sum(txt_raw * txt_raw, axis=1)), "head"
    )
    img_inv = lax.rsqrt(img_sq + 1e-06)[:, None]
    txt_inv = lax.rsqrt(txt_sq + 1e-06)[:, None]
    img_unit = img_raw * img_inv
    txt_unit = txt_raw * txt_inv
    img_emb = img_unit.astype(jnp.bfloat16)
    txt_emb = txt_unit.astype(jnp.bfloat16)
    img_wide, txt_wide = (
        lax.all_gather(img_emb, "head", axis=1, tiled=True),
        lax.all_gather(txt_emb, "head", axis=1, tiled=True),
    )
    offset = lax.axis_index("head") * cols
    piece = lax.all_gather(txt_wide, "dp", axis=0, tiled=True)
    block = lax.dot_general(
        img_wide, piece, (((1,), (1,)), ((), ())), preferred_element_type=jnp.float32
    )
    raw_logits = block
    share = lax.dynamic_slice_in_dim(piece, offset, cols, 1)
    columns = share
    raw_logits, text_cols = (raw_logits, columns)
    logits = logit_scale * raw_logits
    row_lse = jax.nn.logsumexp(logits, axis=1, keepdims=True)
    col_max = jnp.max(logits, axis=0)
    col_sum = jnp.sum(jnp.exp(logits - col_max[None, :]), axis=0)
    top, summed = merged((col_max, col_sum), "dp", combine_totals)
    col_lse = top + jnp.log(summed)
    first = lax.axis_index("dp") * rows
    ident = (
        lax.broadcasted_iota(jnp.int32, logits.shape, 0) + first
        == lax.broadcasted_iota(jnp.int32, logits.shape, 1)
    ).astype(jnp.float32)
    factor = 1.0 / (2.0 * jnp.sqrt(jnp.float32(total)))
    grad_logits = (
        (jnp.exp(logits - row_lse) + jnp.exp(logits - col_lse[None, :]) - 2.0 * ident) * factor
    ).astype(jnp.bfloat16)
    img_demb = logit_scale * jnp.dot(grad_logits, text_cols, preferred_element_type=jnp.float32)
    block = grad_logits
    txt_demb = lax.psum_scatter(
        logit_scale
        * lax.dot_general(
            block, img_emb, (((0,), (0,)), ((), ())), preferred_element_type=jnp.float32
        ),
        "dp",
        scatter_dimension=0,
        tiled=True,
    )
    img_inner, txt_inner = lax.psum(
        (jnp.sum(img_unit * img_demb, axis=1), jnp.sum(txt_unit * txt_demb, axis=1)), "head"
    )
    img_draw = (img_inv * (img_demb - img_unit * img_inner[:, None])).astype(jnp.bfloat16)
    txt_draw = (txt_inv * (txt_demb - txt_unit * txt_inner[:, None])).astype(jnp.bfloat16)
    share = feat_img.shape[1] // lax.axis_size("dp")
    img_grad = lax.dot_general(
        feat_img, img_draw, (((0,), (0,)), ((), ())), preferred_element_type=jnp.float32
    )
    txt_grad = lax.dot_general(
        feat_txt, txt_draw, (((0,), (0,)), ((), ())), preferred_element_type=jnp.float32
    )
    both = lax.psum_scatter(
        jnp.concatenate([img_grad, txt_grad], axis=1), "dp", scatter_dimension=0, tiled=True
    )
    return (both[:, :cols], both[:, cols:])


def solution(mesh):
    return jax.shard_map(
        per_device,
        mesh=mesh,
        in_specs=(P("dp", None), P("dp", None), P(None, "head"), P(None, "head"), P()),
        out_specs=(P("dp", "head"), P("dp", "head")),
        check_vma=False,
    )
```

profile of v0, /device:TPU:16, one launch (start us, length us, event | category | flops | bytes accessed | tf_op | source)
XLA Modules:
  0.0 2052.5 jit_solution(4352356931893147102)
XLA Ops:
  7.2 1.0 copy-done
  8.3 1.3 multiply_reduce_fusion.3
  9.6 1.5 multiply_reduce_fusion.2
  11.1 7.2 all-reduce.2
  18.4 8.0 all_gather.22
  27.2 7.4 all_gather.21
  34.6 367.8 %all-gather.6.cloned.1.call-done = bf16[8192,1024]{1,0:T(8,128)(2,1)} async-done(((bf16[128,1024]{1,0:T(8,128)(2,1)}), bf16[8192,1024]{1,0:T(8,128)(2,1)}) %all-gather.6.cloned.1.call-update) | async-done | bytes 16777232 | tf_op jit(solution)/shard_map/all_gather | solution.py:42
  402.4 13.4 fusion.10
  415.8 4.1 exponential_reduce_fusion.1
  420.7 297.4 %all-gather.10.cloned.1.call-done = f32[524288]{0:T(1024)} async-done(((f32[8192]{0:T(1024)}), f32[524288]{0:T(1024)}) %all-gather.10.cloned.1.call-update) | async-done | bytes 2097168 | tf_op jit(solution)/shard_map/all_gather | solution.py:8
  718.1 1.8 reshape.27
  719.9 297.3 %all-gather.8.cloned.1.call-done = f32[524288]{0:T(1024)} async-done(((f32[8192]{0:T(1024)}), f32[524288]{0:T(1024)}) %all-gather.8.cloned.1.call-update) | async-done | bytes 2097168 | tf_op jit(solution)/shard_map/all_gather | solution.py:8
  1017.2 2.8 reshape.26
  1020.0 67.1 %while.17 = (s32[]{:T(128)}, f32[8192]{0:T(1024)S(1)}, f32[8192]{0:T(1024)S(1)}, f32[64,8192]{1,0:T(8,128)}, f32[64,8192]{1,0:T(8,128)S(1)}, /*index=5*/s32[]{:T(128)}, s32[]{:T(128)}, s32[]{:T(128)}) while((s32[]{:T(128)}, f32[8192]{0:T(1024)S(1)}, f32[8192]{0:T(1024)S(1)}, f32[64,8192]{1,0:T(8,128)}, f32[64,8192]{1,0:T(8,128)S(1)}, ...), condition=%wide.region_9.0_spmd, body=%wide.region_8.0_spmd.sunk | while | flops 49157 | bytes 327811 | solution.py:14
  1021.0 1.0 constant_dynamic-slice_fusion.4
  1022.1 1.0 constant_dynamic-slice_fusion.4
  1023.2 1.0 constant_dynamic-slice_fusion.4
  1024.2 1.0 constant_dynamic-slice_fusion.4
  1027.4 1.0 constant_dynamic-slice_fusion.4
  1028.5 1.0 constant_dynamic-slice_fusion.4
  1029.6 1.0 constant_dynamic-slice_fusion.4
  1030.6 1.0 constant_dynamic-slice_fusion.4
  1034.9 1.0 constant_dynamic-slice_fusion.4
  1036.0 1.0 constant_dynamic-slice_fusion.4
  1037.0 1.0 constant_dynamic-slice_fusion.4
  1041.3 1.0 constant_dynamic-slice_fusion.4
  1042.4 1.0 constant_dynamic-slice_fusion.4
  1043.4 1.0 constant_dynamic-slice_fusion.4
  1044.5 1.0 constant_dynamic-slice_fusion.4
  1047.7 1.0 constant_dynamic-slice_fusion.4
  1048.7 1.0 constant_dynamic-slice_fusion.4
  1049.8 1.0 constant_dynamic-slice_fusion.4
  1050.9 1.0 constant_dynamic-slice_fusion.4
  1055.1 1.0 constant_dynamic-slice_fusion.4
  1056.2 1.0 constant_dynamic-slice_fusion.4
  1057.3 1.0 constant_dynamic-slice_fusion.4
  1061.5 1.0 constant_dynamic-slice_fusion.4
  1062.6 1.0 constant_dynamic-slice_fusion.4
  1063.7 1.0 constant_dynamic-slice_fusion.4
  1087.1 7.8 convolution_multiply_fusion
  1095.2 5.4 multiply_reduce_fusion.1
  1100.7 325.0 %reduce-scatter.3.cloned.1.call-done = f32[128,256]{1,0:T(8,128)} async-done(((f32[8192,256]{1,0:T(8,128)}), f32[128,256]{1,0:T(8,128)}) %reduce-scatter.3.cloned.1.call-update) | async-done | bytes 131088 | tf_op jit(solution)/shard_map/reduce_scatter | solution.py:67
  1425.7 1.1 multiply_reduce_fusion
  1426.7 7.3 all-reduce.1
  1434.5 1.3 convolution_bitcast_fusion
  1435.8 1.7 pad_maximum_fusion
  1438.8 604.7 %all-reduce.5.cloned.1.call-done = f32[1280,512]{0,1:T(8,128)} async-done(((f32[1280,512]{0,1:T(8,128)}), f32[1280,512]{0,1:T(8,128)}) %all-reduce.5.cloned.1.call-update) | async-done | bytes 2621456
  2043.5 1.2 fusion.11
  (136 shorter events, 44.3 us)
Async XLA Ops:
  7.2 1.1 copy-start
  7.2 395.2 %all-gather.6.cloned.1.call-start = ((), (), s32[]{:S(2)}) async-start(), calls=%async_computation.1 | async-start | bytes 17039360 | tf_op jit(solution)/shard_map/all_gather | solution.py:42
  26.4 691.7 %all-gather.10.cloned.1.call-start = ((), (), s32[]{:S(2)}) async-start(), calls=%async_computation.4 | async-start | bytes 2129920 | tf_op jit(solution)/shard_map/all_gather | solution.py:8
  415.8 4.2 copy-start.3
  419.9 597.2 %all-gather.8.cloned.1.call-start = ((), (), s32[]{:S(2)}) async-start(), calls=%async_computation.3 | async-start | bytes 2129920 | tf_op jit(solution)/shard_map/all_gather | solution.py:8
  420.7 1005.0 %reduce-scatter.3.cloned.1.call-start = ((), (), s32[]{:S(2)}) async-start(), calls=%async_computation.2 | async-start | bytes 8519680 | tf_op jit(solution)/shard_map/reduce_scatter | solution.py:67
  718.1 301.9 %slice-start = ((f32[524288]{0:T(1024)}), f32[8192]{0:T(1024)S(1)}, s32[]{:S(2)}) async-start(f32[524288]{0:T(1024)} %all-gather.10.cloned.1.call-done), calls=%async_computation.6 | async-start | bytes 65536 | tf_op jit(solution)/shard_map/slice | solution.py:9
  1017.2 2.8 slice-start.1
  1095.0 948.5 %all-reduce.5.cloned.1.call-start = ((), (), s32[]{:S(2)}) async-start(), calls=%async_computation.5 | async-start | bytes 5242880
  1095.2 338.8 %copy-start.1 = (bf16[128,1280]{1,0:T(8,128)(2,1)S(1)}, bf16[128,1280]{1,0:T(8,128)(2,1)}, u32[]{:S(2)}) copy-start(bf16[128,1280]{1,0:T(8,128)(2,1)} %param.7) | copy-start | bytes 983044
  1095.2 339.3 %copy-start.2 = (bf16[128,1280]{1,0:T(8,128)(2,1)S(1)}, bf16[128,1280]{1,0:T(8,128)(2,1)}, u32[]{:S(2)}) copy-start(bf16[128,1280]{1,0:T(8,128)(2,1)} %param.8) | copy-start | bytes 983044
  1435.8 1.7 copy-start.4
Sparse Core Ops, SparseCore 0:
  26.6 375.8 all-gather.5
  420.0 298.0 all-gather.9
  719.9 297.1 all-gather.7
  1095.1 330.5 reduce-scatter.2
  1437.7 605.7 all-reduce.4
where the time goes:
time: 2060 us; the launch traced here: 2050 us
  waiting for transfers between devices  1890 us (92%)
  local copies, waits for them, and re-layouts  71.9 us (3%)
  matrix products  31.3 us (2%)
  blocking collectives  29.8 us (1%)
    unnamed x6, waiting for transfers between devices  605 us
    all_gather x2, waiting for transfers between devices, merged(): everything = jax.tree.map(lambda part: lax.all_gather(part, axis), array)  595 us
    all_gather x1, waiting for transfers between devices, per_device(): piece = lax.all_gather(txt_wide, 'dp', axis=0, tiled=True)  368 us
    reduce_scatter x1, waiting for transfers between devices, per_device(): lax.psum_scatter(logit_scale * lax.dot_general(block, img_emb, (((0,), (0...  325 us
    dynamic_slice x63, local copies, waits for them, and re-layouts, step(): return combine(so_far, jax.tree.map(lambda part: part[k], everything))  63.2 us
  transfers between devices with their start and end apart: 5, of which 5 were waited for; matrix products, arithmetic and copies ran while one was open for 0% of the time, Pallas kernels for 0%

commit v1 on v0

v1 whole, which is shorter than its diff:
```python
import functools

import jax
import jax.numpy as jnp
from jax import lax
from jax.experimental import pallas as pl
from jax.experimental.pallas import tpu as pltpu
from jax.sharding import PartitionSpec as P

MESH = pl.DeviceIdType.MESH
F32 = jnp.float32
BF16 = jnp.bfloat16


def device(x, y, z, core):
    return {"dp": (x * 8 + z) * 2 + y % 2, "head": (y // 2) * 2 + core}


def place():
    d = lax.axis_index("dp")
    h = lax.axis_index("head")
    return d // 16, (h // 2) * 2 + d % 2, (d // 2) % 8, h % 2


def plane_peer(k):
    x, y, z, core = place()
    return device((x + k % 4) % 4, (y + k // 4) % 4, z, core)


def line_peer(k):
    x, y, z, core = place()
    return device(x, y, (z + k % 8) % 8, (core + k // 8) % 2)


def head_peer(k):
    h = lax.axis_index("head")
    return {"dp": lax.axis_index("dp"), "head": (h + k) % 4}


def send(src, dst, send_sem, recv_sem, peer):
    pltpu.make_async_remote_copy(
        src_ref=src, dst_ref=dst, send_sem=send_sem, recv_sem=recv_sem,
        device_id=peer, device_id_type=MESH,
    ).start()


def drain(ref, sem):
    pltpu.make_async_copy(ref, ref, sem).wait()


def each(lo, hi, body):
    def step(k, carry):
        body(k)
        return carry
    lax.fori_loop(lo, hi, step, 0)


def to_column(row):
    eye = lax.broadcasted_iota(jnp.int32, (128, 128), 0) == lax.broadcasted_iota(jnp.int32, (128, 128), 1)
    return jnp.concatenate(
        [jnp.sum(jnp.where(eye, row[:, 128 * k:128 * k + 128], 0.0), axis=1, keepdims=True)
         for k in range(row.shape[1] // 128)], axis=0)


def lse_rows(a):
    top = jnp.max(a, axis=0, keepdims=True)
    return top + jnp.log(jnp.sum(jnp.exp(a - top), axis=0, keepdims=True))


def put_stats(ref, lse, inv):
    for k in range(4):
        ref[k:k + 1, :] = lse[:, 128 * k:128 * k + 128]
    pick = lax.broadcasted_iota(jnp.int32, (32, 128), 0) == lax.broadcasted_iota(jnp.int32, (32, 128), 1)
    ref[4:5, :] = jnp.sum(jnp.where(pick, inv, 0.0), axis=0, keepdims=True)


def merged_stats(ref):
    a = ref[:, 0:4, :]
    top = jnp.max(a, axis=0)
    lse = top + jnp.log(jnp.sum(jnp.exp(a - top[None]), axis=0))
    lse = jnp.concatenate([lse[k:k + 1, :] for k in range(4)], axis=1)
    inv = jnp.concatenate([ref[k, 4:5, 0:32] for k in range(16)], axis=1)
    return lse, inv


def kernel(scale_ref, fi_ref, ft_ref, wi_ref, wt_ref, oi_ref, ot_ref,
           raw_s, raw_r, emb_i, emb_t, feat_i, feat_t, emb_it, emb_tt, feat_it, feat_tt,
           stat_i, stat_t, log_a, log_b, dem_i, dem_t, sib_s, sib_r, get_i, get_t,
           par_i, par_t, sum_i, sum_t, out_i, out_t, fin_i, fin_t, ssem, rsem):
    x, y, z, core = place()
    h = lax.axis_index("head")
    slot_i = y * 4 + x
    slot_t = core * 8 + z
    sibling = {"dp": lax.axis_index("dp"), "head": h + 1 - 2 * core}
    self_i = (y % 2) == core
    self_t = (y // 2) == (z // 4)

    bar = pltpu.get_barrier_semaphore()

    def hello(peer):
        pl.semaphore_signal(bar, inc=1, device_id=peer, device_id_type=MESH)

    each(1, 16, lambda k: hello(plane_peer(k)))
    each(1, 16, lambda k: hello(line_peer(k)))
    each(1, 4, lambda k: hello(head_peer(k)))

    def from_i(k):
        return device(k, (y // 2) * 2 + core, z, y % 2)

    def to_i(k):
        return device(k, (y // 2) * 2 + core, z, y % 2)

    def from_t(k):
        return device(x, (z // 4) * 2 + y % 2, (y // 2) * 4 + k, core)

    def to_t(k):
        return device(x, (z // 4) * 2 + y % 2, (y // 2) * 4 + k, core)

    def not_self(flag, k, mine, body):
        @pl.when(jnp.logical_not(flag & (k == mine)))
        def _():
            body()

    each(0, 4, lambda k: not_self(self_i, k, x, lambda: hello(from_i(k))))
    each(0, 4, lambda k: not_self(self_t, k, z % 4, lambda: hello(from_t(k))))

    raw_i = jnp.dot(fi_ref[...], wi_ref[...], preferred_element_type=F32)
    raw_t = jnp.dot(ft_ref[...], wt_ref[...], preferred_element_type=F32)
    for k in range(4):
        raw_s[k, 0:32, :] = raw_i[32 * k:32 * k + 32, :]
        raw_s[k, 32:64, :] = raw_t[32 * k:32 * k + 32, :]

    pl.semaphore_wait(bar, 41 - self_i.astype(jnp.int32) - self_t.astype(jnp.int32))

    def send_raw(k):
        peer = head_peer(k)
        send(raw_s.at[peer["head"]], raw_r.at[h], ssem.at[0], rsem.at[0], peer)

    each(1, 4, send_raw)
    raw_r[h] = raw_s[h]
    own = pl.ds(pl.multiple_of(h * 32, 32), 32)
    feat_i[pl.ds(pl.multiple_of(slot_i * 32, 32), 32), :] = fi_ref[own, :]
    feat_t[pl.ds(pl.multiple_of(slot_t * 32, 32), 32), :] = ft_ref[own, :]
    drain(raw_s.at[pl.ds(0, 3)], rsem.at[0])
    whole_i = jnp.concatenate([raw_r[k, 0:32, :] for k in range(4)], axis=1)
    whole_t = jnp.concatenate([raw_r[k, 32:64, :] for k in range(4)], axis=1)
    inv_i = lax.rsqrt(jnp.sum(whole_i * whole_i, axis=1, keepdims=True) + 1e-06)
    inv_t = lax.rsqrt(jnp.sum(whole_t * whole_t, axis=1, keepdims=True) + 1e-06)
    mine_i = pl.ds(pl.multiple_of(slot_i * 32, 32), 32)
    mine_t = pl.ds(pl.multiple_of(slot_t * 32, 32), 32)
    emb_i[mine_i, :] = (whole_i * inv_i).astype(BF16)
    emb_t[mine_t, :] = (whole_t * inv_t).astype(BF16)

    def spread(group, peer, ref, mine, sem):
        each(1, group, lambda k: send(ref.at[mine], ref.at[mine], ssem.at[sem], rsem.at[sem], peer(k)))

    half = pl.ds(pl.multiple_of(core * 256, 256), 256)
    other = pl.ds(pl.multiple_of((1 - core) * 256, 256), 256)
    spread(8, line_peer, emb_t, mine_t, 1)
    spread(16, plane_peer, emb_i, mine_i, 2)
    drain(emb_t.at[pl.ds(0, 224)], rsem.at[1])
    send(emb_t.at[half], emb_t.at[half], ssem.at[3], rsem.at[3], sibling)
    drain(emb_i.at[pl.ds(0, 480)], rsem.at[2])
    drain(emb_t.at[other], rsem.at[3])
    spread(8, line_peer, feat_t, mine_t, 4)
    spread(16, plane_peer, feat_i, mine_i, 5)

    scale = scale_ref[0, 0]
    nt = (((1,), (1,)), ((), ()))
    log_a[...] = scale * lax.dot_general(emb_i[...], emb_t[...], nt, preferred_element_type=F32)
    log_b[...] = scale * lax.dot_general(emb_t[...], emb_i[...], nt, preferred_element_type=F32)
    put_stats(stat_i.at[slot_i], lse_rows(log_b[...]), inv_i)
    put_stats(stat_t.at[slot_t], lse_rows(log_a[...]), inv_t)
    each(1, 16, lambda k: send(stat_i.at[slot_i], stat_i.at[slot_i], ssem.at[6], rsem.at[6], plane_peer(k)))
    each(1, 16, lambda k: send(stat_t.at[slot_t], stat_t.at[slot_t], ssem.at[7], rsem.at[7], line_peer(k)))
    emb_it[...] = emb_i[...].T
    emb_tt[...] = emb_t[...].T
    drain(stat_i.at[pl.ds(0, 15)], rsem.at[6])
    drain(stat_t.at[pl.ds(0, 15)], rsem.at[7])
    row_lse, invs_i = merged_stats(stat_i)
    col_lse, invs_t = merged_stats(stat_t)

    factor = 1.0 / (2.0 * (64.0 * 2.0 ** 0.5))
    ids0 = lax.broadcasted_iota(jnp.int32, (512, 512), 0)
    ids1 = lax.broadcasted_iota(jnp.int32, (512, 512), 1)
    nn = (((1,), (0,)), ((), ()))

    def grads(log, along, across, slot0, slot1, base, unit):
        a = log[...]
        same = (ids0 // 32 == slot0) & (ids0 - ids1 == 32 * (slot0 - slot1))
        g = (jnp.exp(a - along) + jnp.exp(a - across) - jnp.where(same, 2.0, 0.0)) * factor
        g = g.astype(BF16)
        inner = jnp.sum(g.astype(F32) * a, axis=0, keepdims=True)
        dem = scale * lax.dot_general(base[...], g, nn, preferred_element_type=F32)
        return (dem - unit[...].astype(F32) * inner).astype(BF16)

    dt = grads(log_a, to_column(row_lse), col_lse, slot_i, slot_t, emb_it, emb_tt)
    dem_t[...] = dt.reshape(2, 2, 256, 512)
    send(dem_t.at[:, 1 - core], sib_r, ssem.at[8], rsem.at[8], sibling)
    di = grads(log_b, row_lse, to_column(col_lse), slot_t, slot_i, emb_tt, emb_it)
    dem_i[...] = di.reshape(16, 64, 512)

    def send_i(k):
        peer = ((y + k // 4) % 4) * 4 + (x + k % 4) % 4
        send(dem_i.at[peer], get_i.at[slot_i], ssem.at[9], rsem.at[9], plane_peer(k))

    each(1, 16, send_i)
    get_i[slot_i] = dem_i[slot_i]
    drain(sib_r, rsem.at[8])
    sib_s[...] = (sib_r[...].astype(F32) + dem_t[:, core].astype(F32)).astype(BF16).reshape(8, 64, 512)

    def send_t(k):
        send(sib_s.at[(z + k) % 8], get_t.at[z], ssem.at[10], rsem.at[10], line_peer(k))

    each(1, 8, send_t)
    get_t[z] = sib_s[z]

    drain(feat_t.at[pl.ds(0, 224)], rsem.at[4])
    send(feat_t.at[half], feat_t.at[half], ssem.at[11], rsem.at[11], sibling)
    drain(feat_i.at[pl.ds(0, 480)], rsem.at[5])
    feat_it[...] = feat_i[...].T
    drain(feat_t.at[other], rsem.at[11])
    feat_tt[...] = feat_t[...].T

    drain(get_t.at[pl.ds(0, 7)], rsem.at[10])
    draw_t = (invs_t * jnp.sum(get_t[...].astype(F32), axis=0)).astype(BF16)
    out_t[...] = lax.dot_general(feat_tt[...], draw_t, nt, preferred_element_type=F32)
    for s in range(16):
        for a in range(2):
            rows = [320 * (s % 4) + 40 * (4 * (s // 8) + 2 * g + a) + 20 * ((s // 4) % 2) for g in range(2)]
            par_t[s, 24 * a:24 * a + 20, :] = jnp.concatenate([out_t[r:r + 20, :] for r in rows], axis=1)

    def part_t(k):
        peer = ((y + k // 4) % 4) * 4 + (x + k % 4) % 4
        send(par_t.at[peer], sum_t.at[slot_i], ssem.at[12], rsem.at[12], plane_peer(k))

    each(1, 16, part_t)
    sum_t[slot_i] = par_t[slot_i]

    drain(get_i.at[pl.ds(0, 15)], rsem.at[9])
    draw_i = (invs_i * jnp.sum(get_i[...].astype(F32), axis=0)).astype(BF16)
    out_i[...] = lax.dot_general(feat_it[...], draw_i, nt, preferred_element_type=F32)
    for q in range(16):
        for a in range(2):
            rows = [320 * (2 * g + a) + 40 * (q % 8) + 20 * (q // 8) for g in range(2)]
            par_i[q, 24 * a:24 * a + 20, :] = jnp.concatenate([out_i[r:r + 20, :] for r in rows], axis=1)

    def part_i(k):
        peer = ((core + k // 8) % 2) * 8 + (z + k % 8) % 8
        send(par_i.at[peer], sum_i.at[slot_t], ssem.at[13], rsem.at[13], line_peer(k))

    each(1, 16, part_i)
    sum_i[slot_t] = par_i[slot_t]

    def last(par, sums, fin, recv, flag, mine, slot, to, sem):
        drain(sums.at[pl.ds(0, 15)], recv)
        total = jnp.sum(sums[...], axis=0)
        for k in range(4):
            fin[0, k] = total[24 * (k % 2):24 * (k % 2) + 24, :]

        def one(k):
            not_self(flag, k, mine, lambda: send(fin.at[0, k], fin.at[1, slot], ssem.at[sem], rsem.at[sem], to(k)))

        each(0, 4, one)

        @pl.when(flag)
        def _():
            fin[1, slot] = fin[0, mine]

    def wait_last(fin, flag, sem):
        @pl.when(flag)
        def _():
            drain(fin.at[0, pl.ds(0, 3)], sem)

        @pl.when(jnp.logical_not(flag))
        def _():
            drain(fin.at[0], sem)

    last(par_t, sum_t, fin_t, rsem.at[12], self_t, z % 4, z % 4, to_t, 14)
    last(par_i, sum_i, fin_i, rsem.at[13], self_i, x, x, to_i, 15)

    def finish(o_ref, fin, flag, sem, half_id):
        wait_last(fin, flag, rsem.at[sem])
        for k in range(4):
            lo = fin[1, k, 0:20, 0:64]
            hi = fin[1, k, 0:20, 64:128]
            o_ref[:, 64 * k:64 * k + 64] = jnp.where(half_id == 0, lo, hi)

    finish(ot_ref, fin_t, self_t, 14, (z % 4) // 2)
    finish(oi_ref, fin_i, self_i, 15, x // 2)

    drain(raw_s.at[pl.ds(0, 3)], ssem.at[0])
    drain(emb_t.at[pl.ds(0, 224)], ssem.at[1])
    drain(emb_i.at[pl.ds(0, 480)], ssem.at[2])
    drain(emb_t.at[half], ssem.at[3])
    drain(feat_t.at[pl.ds(0, 224)], ssem.at[4])
    drain(feat_i.at[pl.ds(0, 480)], ssem.at[5])
    drain(stat_i.at[pl.ds(0, 15)], ssem.at[6])
    drain(stat_t.at[pl.ds(0, 15)], ssem.at[7])
    drain(sib_r, ssem.at[8])
    drain(get_i.at[pl.ds(0, 15)], ssem.at[9])
    drain(get_t.at[pl.ds(0, 7)], ssem.at[10])
    drain(feat_t.at[half], ssem.at[11])
    drain(sum_t.at[pl.ds(0, 15)], ssem.at[12])
    drain(sum_i.at[pl.ds(0, 15)], ssem.at[13])
    wait_last(fin_t, self_t, ssem.at[14])
    wait_last(fin_i, self_i, ssem.at[15])


def per_device(feat_img, feat_txt, w_img, w_txt, logit_scale):
    v = pl.BlockSpec(memory_space=pltpu.VMEM)
    out = jax.ShapeDtypeStruct((20, 256), F32)
    vm = pltpu.VMEM
    return pl.pallas_call(
        kernel,
        out_shape=(out, out),
        in_specs=[pl.BlockSpec(memory_space=pltpu.SMEM), v, v, v, v],
        out_specs=(v, v),
        scratch_shapes=[
            vm((4, 64, 256), F32), vm((4, 64, 256), F32),
            vm((512, 1024), BF16), vm((512, 1024), BF16),
            vm((512, 1280), BF16), vm((512, 1280), BF16),
            vm((1024, 512), BF16), vm((1024, 512), BF16),
            vm((1280, 512), BF16), vm((1280, 512), BF16),
            vm((16, 8, 128), F32), vm((16, 8, 128), F32),
            vm((512, 512), F32), vm((512, 512), F32),
            vm((16, 64, 512), BF16), vm((2, 2, 256, 512), BF16),
            vm((8, 64, 512), BF16), vm((2, 256, 512), BF16),
            vm((16, 64, 512), BF16), vm((8, 64, 512), BF16),
            vm((16, 48, 128), F32), vm((16, 48, 128), F32),
            vm((16, 48, 128), F32), vm((16, 48, 128), F32),
            vm((1280, 64), F32), vm((1280, 64), F32),
            vm((2, 4, 24, 128), F32), vm((2, 4, 24, 128), F32),
            pltpu.SemaphoreType.DMA((16,)), pltpu.SemaphoreType.DMA((16,)),
        ],
        compiler_params=pltpu.CompilerParams(
            collective_id=0, has_side_effects=True, vmem_limit_bytes=56 * 2 ** 20),
        name="contrastive",
    )(logit_scale.reshape(1, 1), feat_img, feat_txt, w_img, w_txt)


def solution(mesh):
    return jax.shard_map(
        per_device,
        mesh=mesh,
        in_specs=(P("dp", None), P("dp", None), P(None, "head"), P(None, "head"), P()),
        out_specs=(P("dp", "head"), P("dp", "head")),
        check_vma=False,
    )
```

time: 2060 us -> 95.1 us (0.05)
  the two profiles are of different devices: /device:TPU:16 before, /device:TPU:1 now
where the time goes in v1:
time: 95.1 us; the launch traced here: 94.9 us
  Pallas kernels  91.7 us (96%)
  local copies, waits for them, and re-layouts  1.96 us (2%)
  between operations  1.29 us (1%)
    pallas_call x1, Pallas kernels, per_device(): pl.pallas_call(kernel, out_shape=(out, out), in_specs=[pl.BlockSpec(memor...  91.7 us
    unnamed x4, local copies, waits for them, and re-layouts  1.96 us

profile of v1, /device:TPU:1, one launch (start us, length us, event | category | flops | bytes accessed | tf_op | source)
XLA Modules:
  0.0 94.9 jit_solution(16737293694051943458)
XLA Ops:
  1.3 91.7 %contrastive.1 = (f32[20,256]{1,0:T(8,128)}, f32[20,256]{1,0:T(8,128)}) custom-call(f32[1,1]{1,0:T(1,128)} %bitcast.1.scale_ref, bf16[128,1280]{1,0:T(8,128)(2,1)} %fi_ref.1, bf16[128,1280]{1,0:T(8,128)(2,1)} %ft_ref.1, bf16[1280,256]{1,0:T(8,128)(2,1)} %wi_ref.1, bf16[1280,256]{1,0:T(8,128)(2,1)} %wt_ref.1), custom_call_target="tpu_custom_call" | custom-call | tf_op jit(solution)/shard_map/contrastive/pallas_call | solution.py:314
  93.0 0.0 copy-start
  93.0 1.4 %copy.10 = f32[20,256]{1,0:T(8,128)} copy(f32[20,256]{1,0:T(8,128)} %get-tuple-element.4) | data formatting | bytes 40960
  94.3 0.0 copy-done
  94.3 0.6 copy.11
Async XLA Ops:
  93.0 1.4 %copy-start = (f32[20,256]{1,0:T(8,128)S(1)}, f32[20,256]{1,0:T(8,128)}, u32[]{:S(2)}) copy-start(f32[20,256]{1,0:T(8,128)} %get-tuple-element.5) | copy-start | bytes 61444

commit v2 on v1

v2 whole, which is shorter than its diff:
```python
import jax
import jax.numpy as jnp
from jax import lax
from jax.experimental import pallas as pl
from jax.experimental.pallas import tpu as pltpu
from jax.sharding import PartitionSpec as P

MESH = pl.DeviceIdType.MESH
F32 = jnp.float32
BF16 = jnp.bfloat16
NT = (((1,), (1,)), ((), ()))
NN = (((1,), (0,)), ((), ()))


def device(x, y, z, core):
    x, y, z = (x + 4) % 4, (y + 4) % 4, (z + 8) % 8
    return {"dp": (x * 8 + z) * 2 + y % 2, "head": (y // 2) * 2 + core}


def place():
    d = lax.axis_index("dp")
    h = lax.axis_index("head")
    return d // 16, (h // 2) * 2 + d % 2, (d // 2) % 8, h % 2


def image_slot(x, y):
    x, y = (x + 4) % 4, (y + 4) % 4
    return (y % 2) * 8 + x * 2 + y // 2


def text_slot(z, core):
    z = (z + 8) % 8
    return (z // 4) * 8 + core * 4 + z % 4


def rows(slot, count=32, shift=0):
    return pl.ds(pl.multiple_of(slot * 32 + shift, 16), count)


def drain(ref, sem):
    pltpu.make_async_copy(ref, ref, sem).wait()


def each(lo, hi, body):
    def step(k, carry):
        body(k)
        return carry
    lax.fori_loop(lo, hi, step, 0)


def to_column(row):
    eye = lax.broadcasted_iota(jnp.int32, (128, 128), 0) == lax.broadcasted_iota(jnp.int32, (128, 128), 1)
    return jnp.concatenate(
        [jnp.sum(jnp.where(eye, row[:, 128 * k:128 * k + 128], 0.0), axis=1, keepdims=True)
         for k in range(row.shape[1] // 128)], axis=0)


def lse_rows(a):
    top = jnp.max(a, axis=0, keepdims=True)
    return top + jnp.log(jnp.sum(jnp.exp(a - top), axis=0, keepdims=True))


def put_stats(ref, lse, inv):
    for k in range(4):
        ref[k:k + 1, :] = lse[:, 128 * k:128 * k + 128]
    pick = lax.broadcasted_iota(jnp.int32, (32, 128), 0) == lax.broadcasted_iota(jnp.int32, (32, 128), 1)
    ref[4:5, :] = jnp.sum(jnp.where(pick, inv, 0.0), axis=0, keepdims=True)


def merged_stats(ref):
    a = ref[:, 0:4, :]
    top = jnp.max(a, axis=0)
    lse = top + jnp.log(jnp.sum(jnp.exp(a - top[None]), axis=0))
    lse = jnp.concatenate([lse[k:k + 1, :] for k in range(4)], axis=1)
    inv = jnp.concatenate([ref[k, 4:5, 0:32] for k in range(16)], axis=1)
    return lse, inv


def kernel(scale_ref, fi_ref, ft_ref, wi_ref, wt_ref, oi_ref, ot_ref,
           raw_s, raw_r, emb_i, emb_t, feat_i, feat_t, emb_it, emb_tt, feat_it, feat_tt,
           stat_i, stat_t, log_a, log_b, dem_i, dem_t, sib_s, sib_r, get_i, get_t,
           par_i, par_t, sum_i, sum_t, out_s, out_r, fin_i, fin_t, ssem, rsem):
    x, y, z, core = place()
    h = lax.axis_index("head")
    slot_i = image_slot(x, y)
    slot_t = text_slot(z, core)
    sibling = device(x, y, z, 1 - core)
    due = {}
    sent = {}

    def send(src, dst, sem, peer, arrival=None):
        pltpu.make_async_remote_copy(
            src_ref=src, dst_ref=dst, send_sem=ssem.at[sem], recv_sem=rsem.at[sem if arrival is None else arrival],
            device_id=peer, device_id_type=MESH,
        ).start()

    def arrive(i):
        drain(due.pop(i), rsem.at[i])

    def head_peer(k):
        return {"dp": lax.axis_index("dp"), "head": (h + k) % 4}

    def plane_peer(k):
        return device(x + k % 4, y + k // 4, z, core)

    def line_peer(k):
        return device(x, y, z + k % 8, (core + k // 8) % 2)

    self_i = (z % 2 == x // 2) & (core == x % 2) & (core == x // 2)
    self_t = (y == z // 2) & (core == y // 2) & ((z % 4) // 2 == core)
    quarter = (z % 2) * 2 + y % 2

    def to_i(e):
        return device((z % 2) * 2 + core, (y // 2) * 2 + e % 2, (z // 2) * 2 + e // 2, x // 2)

    def to_t(e):
        return device(x, core * 2 + e % 2, 2 * y + e // 2, (z % 4) // 2)

    bar = pltpu.get_barrier_semaphore()

    def hello(peer):
        pl.semaphore_signal(bar, inc=1, device_id=peer, device_id_type=MESH)

    each(1, 4, lambda k: hello(head_peer(k)))
    each(1, 4, lambda k: hello(device(x + k, y, z, core)))
    hello(device(x, y + 1, z, core))
    hello(device(x, y - 1, z, core))
    each(1, 4, lambda k: hello(device(x, y, z + k, core)))
    each(1, 4, lambda k: hello(device(x, y, z - k, core)))

    raw_i = jnp.dot(fi_ref[...].reshape(128, 1280), wi_ref[...], preferred_element_type=F32)
    for k in range(4):
        raw_s[0, k] = raw_i[32 * k:32 * k + 32, :]
    raw_t = jnp.dot(ft_ref[...].reshape(128, 1280), wt_ref[...], preferred_element_type=F32)
    for k in range(4):
        raw_s[1, k] = raw_t[32 * k:32 * k + 32, :]

    pl.semaphore_wait(bar, 14)

    def send_raw(side, sem):
        def one(k):
            peer = head_peer(k)
            send(raw_s.at[side, peer["head"]], raw_r.at[side, h], sem, peer)
        each(1, 4, one)
        due[sem] = sent[sem] = raw_s.at[side, pl.ds(0, 3)]
        raw_r[side, h] = raw_s[side, h]

    send_raw(0, 0)
    send_raw(1, 1)

    each(1, 4, lambda k: send(fi_ref.at[:, core], feat_i.at[x], 2, device(x + k, y, z, core)))
    due[2] = sent[2] = feat_i.at[pl.ds(0, 3)]
    feat_i[x] = fi_ref[:, core]
    each(1, 4, lambda k: send(ft_ref.at[y // 2, core], feat_t.at[core, z % 4], 3,
                              device(x, y, (z // 4) * 4 + (z + k) % 4, core)))
    due[3] = sent[3] = feat_t.at[0, pl.ds(0, 3)]
    feat_t[core, z % 4] = ft_ref[y // 2, core]

    def unit_rows(side):
        whole = jnp.concatenate([raw_r[side, k] for k in range(4)], axis=1)
        inv = lax.rsqrt(jnp.sum(whole * whole, axis=1, keepdims=True) + 1e-06)
        return (whole * inv).astype(BF16), inv

    order = (1, 3, 2)
    mine_i = rows(slot_i)
    mine_t = rows(slot_t)
    arrive(0)
    unit_i, inv_i = unit_rows(0)
    emb_i[mine_i, :] = unit_i
    for k in order:
        send(emb_i.at[mine_i], emb_i.at[mine_i], 4, device(x + k, y, z, core), 4 + k)
        send(emb_i.at[mine_i], emb_i.at[mine_i], 4, device(x, y + k, z, core), 7 + k)
        due[4 + k] = due[7 + k] = emb_i.at[rows(0)]
    sent[4] = emb_i.at[rows(0, 480)]
    due[11] = emb_i.at[rows(0, 288)]
    arrive(1)
    unit_t, inv_t = unit_rows(1)
    emb_t[mine_t, :] = unit_t
    for k, s in enumerate((2, -2, 1, -1)):
        send(emb_t.at[mine_t], emb_t.at[mine_t], 12, device(x, y, z + s, core), 12 + k)
        due[12 + k] = emb_t.at[rows(0)]
    sent[12] = emb_t.at[rows(0, 224)]
    due[16] = emb_t.at[rows(0, 96)]

    def forward_x(k):
        arrive(4 + k)
        block = rows(image_slot(x - k, y), 16)
        for j in order:
            send(emb_i.at[block], emb_i.at[block], 4, device(x, y + j, z, core), 11)

    def forward_y(k):
        arrive(7 + k)
        block = rows(image_slot(x, y - k), 16, 16)
        for j in order:
            send(emb_i.at[block], emb_i.at[block], 4, device(x + j, y, z, core), 11)

    def forward_z(k, s):
        arrive(12 + k)
        block = rows(text_slot(z + 2 * s, core))
        send(emb_t.at[block], emb_t.at[block], 12, device(x, y, z - s, core), 16)
        block = rows(text_slot(z + 2 * s, core), 16, 16 * k)
        send(emb_t.at[block], emb_t.at[block], 12, device(x, y, z - 2 * s, core), 16)

    forward_x(1)
    forward_y(1)
    forward_x(3)
    forward_y(3)
    forward_x(2)
    forward_y(2)
    forward_z(0, -1)
    forward_z(1, 1)
    arrive(14)
    arrive(15)
    arrive(16)
    for k in range(2):
        part = pl.ds(pl.multiple_of(256 * k + 128 * core, 128), 128)
        send(emb_t.at[part], emb_t.at[part], 17, sibling)
    due[17] = sent[17] = emb_t.at[pl.ds(0, 256)]
    arrive(11)
    arrive(17)

    scale = scale_ref[0, 0]
    log_a[...] = scale * lax.dot_general(emb_i[...], emb_t[...], NT, preferred_element_type=F32)
    log_b[...] = scale * lax.dot_general(emb_t[...], emb_i[...], NT, preferred_element_type=F32)
    put_stats(stat_i.at[slot_i], lse_rows(log_b[...]), inv_i)
    put_stats(stat_t.at[slot_t], lse_rows(log_a[...]), inv_t)
    each(1, 16, lambda k: send(stat_i.at[slot_i], stat_i.at[slot_i], 18, plane_peer(k)))
    due[18] = sent[18] = stat_i.at[pl.ds(0, 15)]
    each(1, 16, lambda k: send(stat_t.at[slot_t], stat_t.at[slot_t], 19, line_peer(k)))
    due[19] = sent[19] = stat_t.at[pl.ds(0, 15)]
    emb_it[...] = emb_i[...].T
    emb_tt[...] = emb_t[...].T
    arrive(3)
    send(feat_t.at[core], feat_t.at[core], 20, sibling)
    due[20] = sent[20] = feat_t.at[0]
    arrive(2)
    feat_it[...] = feat_i[...].reshape(256, 1280).T
    arrive(18)
    arrive(19)
    row_lse, invs_i = merged_stats(stat_i)
    col_lse, invs_t = merged_stats(stat_t)

    factor = 1.0 / (2.0 * (64.0 * 2.0 ** 0.5))
    ids0 = lax.broadcasted_iota(jnp.int32, (512, 512), 0)
    ids1 = lax.broadcasted_iota(jnp.int32, (512, 512), 1)

    def grads(log, along, across, slot0, slot1, base, unit, dem):
        a = log[...]
        same = (ids0 // 32 == slot0) & (ids0 - ids1 == 32 * (slot0 - slot1))
        g = (jnp.exp(a - along) + jnp.exp(a - across) - jnp.where(same, 2.0, 0.0)) * factor
        g = g.astype(BF16)
        inner = jnp.sum(g.astype(F32) * a, axis=0, keepdims=True)
        d = scale * lax.dot_general(base[...], g, NN, preferred_element_type=F32)
        d = (d - unit[...].astype(F32) * inner).astype(BF16)
        for k in range(2):
            dem[k] = d[:, 256 * k:256 * k + 256].reshape(8, 128, 256)

    grads(log_a, to_column(row_lse), col_lse, slot_i, slot_t, emb_it, emb_tt, dem_t)
    send(dem_t.at[:, pl.ds(4 - 4 * core, 4)], sib_r, 21, sibling)
    due[21] = sent[21] = sib_r
    grads(log_b, row_lse, to_column(col_lse), slot_t, slot_i, emb_tt, emb_it, dem_i)

    def send_i(k):
        px, py = (x + k % 4) % 4, (y + k // 4) % 4
        send(dem_i.at[py % 2, (py // 2) * 4 + px], get_i.at[slot_i], 22, plane_peer(k))

    each(1, 16, send_i)
    due[22] = sent[22] = get_i.at[pl.ds(0, 15)]
    get_i[slot_i] = dem_i[y % 2, (y // 2) * 4 + x]
    arrive(21)
    own = dem_t[:, pl.ds(4 * core, 4)]
    sib_s[...] = (sib_r[...].astype(F32) + own.astype(F32)).astype(BF16).reshape(8, 128, 256)

    def send_t(k):
        send(sib_s.at[(z + k) % 8], get_t.at[z], 23, line_peer(k))

    each(1, 8, send_t)
    due[23] = sent[23] = get_t.at[pl.ds(0, 7)]
    get_t[z] = sib_s[z]
    arrive(20)
    feat_tt[...] = feat_t[...].reshape(256, 1280).T

    def weights(get, invs, upper, feats):
        inv = jnp.where(upper, invs[:, 256:512], invs[:, 0:256])
        draw = inv * jnp.sum(get[...].astype(F32), axis=0)
        high = draw.astype(BF16)
        low = (draw - high.astype(F32)).astype(BF16)
        f = feats[...]
        out = lax.dot_general(f, high, NT, preferred_element_type=F32)
        out += lax.dot_general(f, low, NT, preferred_element_type=F32)
        return out.reshape(16, 80, 128)

    arrive(23)
    par_t[...] = weights(get_t, invs_t, z // 4 == 1, feat_tt).astype(BF16)

    def part_t(k):
        px, py = (x + k % 4) % 4, (y + k // 4) % 4
        send(par_t.at[px * 4 + py], sum_t.at[slot_i], 24, plane_peer(k))

    each(1, 16, part_t)
    due[24] = sent[24] = sum_t.at[pl.ds(0, 15)]
    sum_t[slot_i] = par_t[x * 4 + y]

    arrive(22)
    def chunk_i(pz, pc):
        return ((pz % 2) * 2 + pc) * 4 + pz // 2

    par_i[...] = weights(get_i, invs_i, y % 2 == 1, feat_it)
    for k in range(8):
        out_s[k] = par_i[chunk_i(k, 1 - core)]
    send(out_s, out_r, 25, sibling)
    due[25] = sent[25] = out_r
    arrive(25)
    for k in range(8):
        par_t_i = par_i[chunk_i(k, core)] + out_r[k]
        sib_p = par_t_i.astype(BF16)
        sum_i[8 + k] = sib_p

    def part_i(k):
        send(sum_i.at[8 + (z + k) % 8], sum_i.at[z], 26, line_peer(k))

    each(1, 8, part_i)
    due[26] = sent[26] = sum_i.at[pl.ds(0, 7)]
    sum_i[z] = sum_i[8 + z]

    def last(total, fin, flag, slot, to, sem):
        for k in range(4):
            fin[0, k, 0:20, :] = total[20 * k:20 * k + 20, :]

        def one(k):
            @pl.when(jnp.logical_not(flag & (k == quarter)))
            def _():
                send(fin.at[0, k], fin.at[1, slot], sem, to(k))

        each(0, 4, one)

        @pl.when(flag)
        def _():
            fin[1, slot] = fin[0, quarter]

    def wait_last(fin, flag, sem):
        @pl.when(flag)
        def _():
            drain(fin.at[0, pl.ds(0, 3)], sem)

        @pl.when(jnp.logical_not(flag))
        def _():
            drain(fin.at[0], sem)

    arrive(24)
    last(jnp.sum(sum_t[...].astype(F32), axis=0), fin_t, self_t, (z // 4) * 2 + z % 2, to_t, 27)
    arrive(26)
    last(jnp.sum(sum_i[0:8].astype(F32), axis=0), fin_i, self_i, (y % 2) * 2 + x % 2, to_i, 28)

    def finish(o_ref, fin, flag, sem):
        wait_last(fin, flag, rsem.at[sem])
        for k in range(2):
            o_ref[:, 128 * k:128 * k + 128] = fin[1, k, 0:20, :] + fin[1, 2 + k, 0:20, :]

    finish(ot_ref, fin_t, self_t, 27)
    finish(oi_ref, fin_i, self_i, 28)

    for i, ref in sent.items():
        drain(ref, ssem.at[i])
    wait_last(fin_t, self_t, ssem.at[27])
    wait_last(fin_i, self_i, ssem.at[28])


def per_device(feat_img, feat_txt, w_img, w_txt, logit_scale):
    v = pl.BlockSpec(memory_space=pltpu.VMEM)
    out = jax.ShapeDtypeStruct((20, 256), F32)
    vm = pltpu.VMEM
    return pl.pallas_call(
        kernel,
        out_shape=(out, out),
        in_specs=[pl.BlockSpec(memory_space=pltpu.SMEM), v, v, v, v],
        out_specs=(v, v),
        scratch_shapes=[
            vm((2, 4, 32, 256), F32), vm((2, 4, 32, 256), F32),
            vm((512, 1024), BF16), vm((512, 1024), BF16),
            vm((4, 2, 32, 1280), BF16), vm((2, 4, 32, 1280), BF16),
            vm((1024, 512), BF16), vm((1024, 512), BF16),
            vm((1280, 256), BF16), vm((1280, 256), BF16),
            vm((16, 8, 128), F32), vm((16, 8, 128), F32),
            vm((512, 512), F32), vm((512, 512), F32),
            vm((2, 8, 128, 256), BF16), vm((2, 8, 128, 256), BF16),
            vm((8, 128, 256), BF16), vm((2, 4, 128, 256), BF16),
            vm((16, 128, 256), BF16), vm((8, 128, 256), BF16),
            vm((16, 80, 128), F32), vm((16, 80, 128), BF16),
            vm((16, 80, 128), BF16), vm((16, 80, 128), BF16),
            vm((8, 80, 128), F32), vm((8, 80, 128), F32),
            vm((2, 4, 24, 128), F32), vm((2, 4, 24, 128), F32),
            pltpu.SemaphoreType.DMA((32,)), pltpu.SemaphoreType.DMA((32,)),
        ],
        compiler_params=pltpu.CompilerParams(
            collective_id=0, has_side_effects=True, vmem_limit_bytes=56 * 2 ** 20),
        name="contrastive",
    )(logit_scale.reshape(1, 1), feat_img.reshape(2, 2, 32, 1280), feat_txt.reshape(2, 2, 32, 1280), w_img, w_txt)


def solution(mesh):
    return jax.shard_map(
        per_device,
        mesh=mesh,
        in_specs=(P("dp", None), P("dp", None), P(None, "head"), P(None, "head"), P()),
        out_specs=(P("dp", "head"), P("dp", "head")),
        check_vma=False,
    )
```

time: 95.1 us -> 73 us (0.77)
  Pallas kernels: 91.7 us -> 69.4 us
    pallas_call x1, Pallas kernels: 91.7 us -> 69.4 us  [per_device(): pl.pallas_call(kernel, out_shape=(out, out), in_specs=[pl.BlockSpec(memor...]
where the time goes in v2:
time: 73 us; the launch traced here: 72.7 us
  Pallas kernels  69.4 us (95%)
  local copies, waits for them, and re-layouts  1.96 us (3%)
  between operations  1.29 us (2%)
    pallas_call x1, Pallas kernels, per_device(): pl.pallas_call(kernel, out_shape=(out, out), in_specs=[pl.BlockSpec(memor...  69.4 us
    unnamed x4, local copies, waits for them, and re-layouts  1.96 us

profile of v2, /device:TPU:1, one launch (start us, length us, event | category | flops | bytes accessed | tf_op | source)
XLA Modules:
  0.0 72.7 jit_solution(16334211822504230077)
XLA Ops:
  1.3 69.4 %contrastive.1 = (f32[20,256]{1,0:T(8,128)}, f32[20,256]{1,0:T(8,128)}) custom-call(f32[1,1]{1,0:T(1,128)} %bitcast.3.scale_ref, bf16[2,2,32,1280]{3,2,1,0:T(8,128)(2,1)} %bitcast.4, bf16[2,2,32,1280]{3,2,1,0:T(8,128)(2,1)} %bitcast.5, bf16[1280,256]{1,0:T(8,128)(2,1)} %wi_ref.1, bf16[1280,256]{1,0:T(8,128)(2,1)} %wt_ref.1), custom_call_target="tpu_custom_call" | custom-call | tf_op jit(solution)/shard_map/contrastive/pallas_call | solution.py:373
  70.7 0.0 copy-start
  70.7 1.4 %copy.10 = f32[20,256]{1,0:T(8,128)} copy(f32[20,256]{1,0:T(8,128)} %get-tuple-element.4) | data formatting | bytes 40960
  72.1 0.0 copy-done
  72.1 0.6 copy.11
Async XLA Ops:
  70.7 1.4 %copy-start = (f32[20,256]{1,0:T(8,128)S(1)}, f32[20,256]{1,0:T(8,128)}, u32[]{:S(2)}) copy-start(f32[20,256]{1,0:T(8,128)} %get-tuple-element.5) | copy-start | bytes 61444

commit v3 on v2

--- a/solution.py
+++ b/solution.py
@@ -77,9 +77,11 @@
 
 
 def kernel(scale_ref, fi_ref, ft_ref, wi_ref, wt_ref, oi_ref, ot_ref,
+           fi_v, ft_v, wi_v, wt_v,
            raw_s, raw_r, emb_i, emb_t, feat_i, feat_t, emb_it, emb_tt, feat_it, feat_tt,
-           stat_i, stat_t, log_a, log_b, dem_i, dem_t, sib_s, sib_r, get_i, get_t,
-           par_i, par_t, sum_i, sum_t, out_s, out_r, fin_i, fin_t, ssem, rsem):
+           stat_i, stat_t, log_a, log_b, own_i, dem_x, dem_y, get_x, get_y, dem_x2, dem_y2, last_x, last_y,
+           own_t, dem_t, sib_r, sib_s, full_z, half_z, sum_z, get_t,
+           par_i, par_t, sum_i, sum_t, out_s, out_r, fin_i, fin_t, ssem, rsem, lsem):
     x, y, z, core = place()
     h = lax.axis_index("head")
     slot_i = image_slot(x, y)
@@ -128,12 +130,16 @@
     each(1, 4, lambda k: hello(device(x, y, z + k, core)))
     each(1, 4, lambda k: hello(device(x, y, z - k, core)))
 
-    raw_i = jnp.dot(fi_ref[...].reshape(128, 1280), wi_ref[...], preferred_element_type=F32)
-    for k in range(4):
-        raw_s[0, k] = raw_i[32 * k:32 * k + 32, :]
-    raw_t = jnp.dot(ft_ref[...].reshape(128, 1280), wt_ref[...], preferred_element_type=F32)
-    for k in range(4):
-        raw_s[1, k] = raw_t[32 * k:32 * k + 32, :]
+    fetched = [pltpu.make_async_copy(a, b, lsem.at[k])
+               for k, (a, b) in enumerate(((fi_ref, fi_v), (wi_ref, wi_v), (ft_ref, ft_v), (wt_ref, wt_v)))]
+    for copy in fetched:
+        copy.start()
+
+    for side, (f, w) in enumerate(((fi_v, wi_v), (ft_v, wt_v))):
+        fetched[2 * side].wait()
+        fetched[2 * side + 1].wait()
+        raw = jnp.dot(f[...].reshape(128, 1280), w[...], preferred_element_type=F32)
+        raw_s[side] = raw.reshape(4, 32, 256)
 
     pl.semaphore_wait(bar, 14)
 
@@ -147,14 +153,6 @@
 
     send_raw(0, 0)
     send_raw(1, 1)
-
-    each(1, 4, lambda k: send(fi_ref.at[:, core], feat_i.at[x], 2, device(x + k, y, z, core)))
-    due[2] = sent[2] = feat_i.at[pl.ds(0, 3)]
-    feat_i[x] = fi_ref[:, core]
-    each(1, 4, lambda k: send(ft_ref.at[y // 2, core], feat_t.at[core, z % 4], 3,
-                              device(x, y, (z // 4) * 4 + (z + k) % 4, core)))
-    due[3] = sent[3] = feat_t.at[0, pl.ds(0, 3)]
-    feat_t[core, z % 4] = ft_ref[y // 2, core]
 
     def unit_rows(side):
         whole = jnp.concatenate([raw_r[side, k] for k in range(4)], axis=1)
@@ -171,16 +169,12 @@
         send(emb_i.at[mine_i], emb_i.at[mine_i], 4, device(x + k, y, z, core), 4 + k)
         send(emb_i.at[mine_i], emb_i.at[mine_i], 4, device(x, y + k, z, core), 7 + k)
         due[4 + k] = due[7 + k] = emb_i.at[rows(0)]
-    sent[4] = emb_i.at[rows(0, 480)]
-    due[11] = emb_i.at[rows(0, 288)]
     arrive(1)
     unit_t, inv_t = unit_rows(1)
     emb_t[mine_t, :] = unit_t
     for k, s in enumerate((2, -2, 1, -1)):
         send(emb_t.at[mine_t], emb_t.at[mine_t], 12, device(x, y, z + s, core), 12 + k)
         due[12 + k] = emb_t.at[rows(0)]
-    sent[12] = emb_t.at[rows(0, 224)]
-    due[16] = emb_t.at[rows(0, 96)]
 
     def forward_x(k):
         arrive(4 + k)
@@ -201,20 +195,33 @@
         block = rows(text_slot(z + 2 * s, core), 16, 16 * k)
         send(emb_t.at[block], emb_t.at[block], 12, device(x, y, z - 2 * s, core), 16)
 
+    def to_sibling(z_from):
+        block = rows(text_slot(z_from, core))
+        send(emb_t.at[block], emb_t.at[block], 17, sibling)
+
+    to_sibling(z)
     forward_x(1)
     forward_y(1)
     forward_x(3)
     forward_y(3)
+    forward_z(0, -1)
+    forward_z(1, 1)
     forward_x(2)
     forward_y(2)
-    forward_z(0, -1)
-    forward_z(1, 1)
+    due[11] = emb_i.at[rows(0, 288)]
+    due[16] = emb_t.at[rows(0, 96)]
+    sent[4] = emb_i.at[rows(0, 480)]
+    sent[12] = emb_t.at[rows(0, 224)]
+    to_sibling(z - 2)
+    to_sibling(z + 2)
     arrive(14)
+    to_sibling(z - 1)
     arrive(15)
+    to_sibling(z + 1)
     arrive(16)
-    for k in range(2):
-        part = pl.ds(pl.multiple_of(256 * k + 128 * core, 128), 128)
-        send(emb_t.at[part], emb_t.at[part], 17, sibling)
+    to_sibling(z + 3)
+    to_sibling(z - 3)
+    to_sibling(z + 4)
     due[17] = sent[17] = emb_t.at[pl.ds(0, 256)]
     arrive(11)
     arrive(17)
@@ -228,61 +235,122 @@
     due[18] = sent[18] = stat_i.at[pl.ds(0, 15)]
     each(1, 16, lambda k: send(stat_t.at[slot_t], stat_t.at[slot_t], 19, line_peer(k)))
     due[19] = sent[19] = stat_t.at[pl.ds(0, 15)]
+    each(1, 4, lambda k: send(fi_v.at[:, core], feat_i.at[x], 2, device(x + k, y, z, core)))
+    due[2] = sent[2] = feat_i.at[pl.ds(0, 3)]
+    feat_i[x] = fi_v[:, core]
+    each(1, 4, lambda k: send(ft_v.at[y // 2, core], feat_t.at[core, z % 4], 3,
+                              device(x, y, (z // 4) * 4 + (z + k) % 4, core)))
+    due[3] = sent[3] = feat_t.at[0, pl.ds(0, 3)]
+    feat_t[core, z % 4] = ft_v[y // 2, core]
+
     emb_it[...] = emb_i[...].T
     emb_tt[...] = emb_t[...].T
+    arrive(18)
+    arrive(19)
+    row_lse, invs_i = merged_stats(stat_i)
+    col_lse, invs_t = merged_stats(stat_t)
+
+    factor = 1.0 / (2.0 * (64.0 * 2.0 ** 0.5))
+    ids0 = lax.broadcasted_iota(jnp.int32, (512, 512), 0)
+    ids1 = lax.broadcasted_iota(jnp.int32, (512, 512), 1)
+
+    def grads(log, along, across, slot0, slot1):
+        a = log[...]
+        same = (ids0 // 32 == slot0) & (ids0 - ids1 == 32 * (slot0 - slot1))
+        g = (jnp.exp(a - along) + jnp.exp(a - across) - jnp.where(same, 2.0, 0.0)) * factor
+        g = g.astype(BF16)
+        return g, jnp.sum(g.astype(F32) * a, axis=0, keepdims=True)
+
+    def demb(g, inner, base, unit, half):
+        part = pl.ds(pl.multiple_of(512 * half, 512), 512)
+        d = scale * lax.dot_general(base[part, :], g, NN, preferred_element_type=F32)
+        return d - unit[part, :].astype(F32) * inner
+
+    g, inner = grads(log_a, to_column(row_lse), col_lse, slot_i, slot_t)
+    d = demb(g, inner, emb_it, emb_tt, 1 - core)
+    for k in range(2):
+        dem_t[k] = d[:, 256 * k:256 * k + 256].astype(BF16).reshape(4, 128, 256)
+    send(dem_t, sib_r, 21, sibling)
+    due[21] = sent[21] = sib_r
+    d = demb(g, inner, emb_it, emb_tt, core)
+    for k in range(2):
+        own_t[4 * k:4 * k + 4] = d[:, 256 * k:256 * k + 256].reshape(4, 128, 256)
+
+    g, inner = grads(log_b, row_lse, to_column(col_lse), slot_t, slot_i)
+
+    def image_half(pair):
+        d = demb(g, inner, emb_tt, emb_it, pair)
+        for k in range(2):
+            py = 2 * pair + k
+            e = d[:, 256 * k:256 * k + 256].reshape(4, 2, 64, 256)
+            own_i[py] = e
+            dem_x[:, py] = e[:, 0].astype(BF16)
+            dem_y[py] = e[:, 1].astype(BF16)
+
+    def send_y(py):
+        send(dem_y.at[py], get_y.at[y], 29, device(x, py, z, core))
+
+    image_half(1 - y // 2)
+    send_y((y + 2) % 4)
+    send_y((1 - y // 2) * 2 + (y + 1) % 2)
+    image_half(y // 2)
+    each(0, 3, lambda k: send(dem_x.at[(x + 1 + (k + 1) % 3) % 4], get_x.at[x], 22, device(x + 1 + (k + 1) % 3, y, z, core)))
+    send_y((y // 2) * 2 + (y + 1) % 2)
+    due[22] = sent[22] = get_x.at[pl.ds(0, 3)]
+    due[29] = sent[29] = get_y.at[pl.ds(0, 3)]
+    arrive(21)
+    own_t[...] = own_t[...] + sib_r[...].astype(F32).reshape(8, 128, 256)
+    sib_s[...] = own_t[...].astype(BF16)
+    for k, s in enumerate((1, -1)):
+        far = (z + 4) % 8
+        half = pl.ds(64 * k, 64)
+        send(sib_s.at[far, half], half_z.at[k], 30, device(x, y, z + 2 * s, core))
+        send(sib_s.at[(z + 3 * s + 8) % 8], full_z.at[k], 23, device(x, y, z + s, core))
+        send(sib_s.at[(z + s + 8) % 8], get_t.at[k], 31, device(x, y, z + s, core))
+    due[23] = sent[23] = full_z
+    due[30] = sent[30] = half_z
+
     arrive(3)
     send(feat_t.at[core], feat_t.at[core], 20, sibling)
     due[20] = sent[20] = feat_t.at[0]
     arrive(2)
     feat_it[...] = feat_i[...].reshape(256, 1280).T
-    arrive(18)
-    arrive(19)
-    row_lse, invs_i = merged_stats(stat_i)
-    col_lse, invs_t = merged_stats(stat_t)
-
-    factor = 1.0 / (2.0 * (64.0 * 2.0 ** 0.5))
-    ids0 = lax.broadcasted_iota(jnp.int32, (512, 512), 0)
-    ids1 = lax.broadcasted_iota(jnp.int32, (512, 512), 1)
-
-    def grads(log, along, across, slot0, slot1, base, unit, dem):
-        a = log[...]
-        same = (ids0 // 32 == slot0) & (ids0 - ids1 == 32 * (slot0 - slot1))
-        g = (jnp.exp(a - along) + jnp.exp(a - across) - jnp.where(same, 2.0, 0.0)) * factor
-        g = g.astype(BF16)
-        inner = jnp.sum(g.astype(F32) * a, axis=0, keepdims=True)
-        d = scale * lax.dot_general(base[...], g, NN, preferred_element_type=F32)
-        d = (d - unit[...].astype(F32) * inner).astype(BF16)
-        for k in range(2):
-            dem[k] = d[:, 256 * k:256 * k + 256].reshape(8, 128, 256)
-
-    grads(log_a, to_column(row_lse), col_lse, slot_i, slot_t, emb_it, emb_tt, dem_t)
-    send(dem_t.at[:, pl.ds(4 - 4 * core, 4)], sib_r, 21, sibling)
-    due[21] = sent[21] = sib_r
-    grads(log_b, row_lse, to_column(col_lse), slot_t, slot_i, emb_tt, emb_it, dem_i)
-
-    def send_i(k):
-        px, py = (x + k % 4) % 4, (y + k // 4) % 4
-        send(dem_i.at[py % 2, (py // 2) * 4 + px], get_i.at[slot_i], 22, plane_peer(k))
-
-    each(1, 16, send_i)
-    due[22] = sent[22] = get_i.at[pl.ds(0, 15)]
-    get_i[slot_i] = dem_i[y % 2, (y // 2) * 4 + x]
-    arrive(21)
-    own = dem_t[:, pl.ds(4 * core, 4)]
-    sib_s[...] = (sib_r[...].astype(F32) + own.astype(F32)).astype(BF16).reshape(8, 128, 256)
-
-    def send_t(k):
-        send(sib_s.at[(z + k) % 8], get_t.at[z], 23, line_peer(k))
-
-    each(1, 8, send_t)
-    due[23] = sent[23] = get_t.at[pl.ds(0, 7)]
-    get_t[z] = sib_s[z]
     arrive(20)
     feat_tt[...] = feat_t[...].reshape(256, 1280).T
 
-    def weights(get, invs, upper, feats):
+    arrive(29)
+    for k in range(1, 4):
+        px = (x + k) % 4
+        total = own_i[y, px, 1]
+        for j in range(1, 4):
+            total += get_y[(y + j) % 4, px].astype(F32)
+        dem_y2[px] = total.astype(BF16)
+        send(dem_y2.at[px], last_y.at[x], 32, device(px, y, z, core))
+    due[32] = sent[32] = last_y.at[pl.ds(0, 3)]
+    arrive(22)
+    for k in range(1, 4):
+        py = (y + k) % 4
+        total = own_i[py, x, 0]
+        for j in range(1, 4):
+            total += get_x[(x + j) % 4, py].astype(F32)
+        dem_x2[py] = total.astype(BF16)
+        send(dem_x2.at[py], last_x.at[y], 33, device(x, py, z, core))
+    due[33] = sent[33] = last_x.at[pl.ds(0, 3)]
+    arrive(23)
+    arrive(30)
+    for k, s in enumerate((1, -1)):
+        dest = (z + 2 * s + 8) % 8
+        total = own_t[dest] + full_z[k].astype(F32)
+        extra = half_z[k].astype(F32)
+        blank = jnp.zeros_like(extra)
+        total += jnp.concatenate([extra, blank] if k == 0 else [blank, extra], axis=0)
+        sum_z[k] = total.astype(BF16)
+        send(sum_z.at[k], get_t.at[2 + k], 31, device(x, y, z + 2 * s, core))
+    due[31] = sent[31] = get_t
+
+    def weights(total, invs, upper, feats):
         inv = jnp.where(upper, invs[:, 256:512], invs[:, 0:256])
-        draw = inv * jnp.sum(get[...].astype(F32), axis=0)
+        draw = inv * total
         high = draw.astype(BF16)
         low = (draw - high.astype(F32)).astype(BF16)
         f = feats[...]
@@ -290,22 +358,22 @@
         out += lax.dot_general(f, low, NT, preferred_element_type=F32)
         return out.reshape(16, 80, 128)
 
-    arrive(23)
-    par_t[...] = weights(get_t, invs_t, z // 4 == 1, feat_tt).astype(BF16)
-
-    def part_t(k):
-        px, py = (x + k % 4) % 4, (y + k // 4) % 4
-        send(par_t.at[px * 4 + py], sum_t.at[slot_i], 24, plane_peer(k))
-
-    each(1, 16, part_t)
-    due[24] = sent[24] = sum_t.at[pl.ds(0, 15)]
-    sum_t[slot_i] = par_t[x * 4 + y]
-
-    arrive(22)
+    def image_sum(own, first, lines, last, at):
+        total = own
+        for j in range(1, 4):
+            total += first((at + j) % 4).astype(F32)
+            total += last[(lines + j) % 4].astype(F32)
+        return total
+
+    arrive(32)
+    arrive(33)
     def chunk_i(pz, pc):
         return ((pz % 2) * 2 + pc) * 4 + pz // 2
 
-    par_i[...] = weights(get_i, invs_i, y % 2 == 1, feat_it)
+    upper_cols = image_sum(own_i[y, x, 0], lambda j: get_x[j, y], y, last_x, x)
+    lower_cols = image_sum(own_i[y, x, 1], lambda j: get_y[j, x], x, last_y, y)
+    total_i = jnp.concatenate([upper_cols, lower_cols], axis=0)
+    par_i[...] = weights(total_i, invs_i, y % 2 == 1, feat_it)
     for k in range(8):
         out_s[k] = par_i[chunk_i(k, 1 - core)]
     send(out_s, out_r, 25, sibling)
@@ -323,6 +391,18 @@
     due[26] = sent[26] = sum_i.at[pl.ds(0, 7)]
     sum_i[z] = sum_i[8 + z]
 
+
+    arrive(31)
+    total_t = own_t[z] + jnp.sum(get_t[...].astype(F32), axis=0)
+    par_t[...] = weights(total_t, invs_t, z // 4 == 1, feat_tt).astype(BF16)
+
+    def part_t(k):
+        px, py = (x + k % 4) % 4, (y + k // 4) % 4
+        send(par_t.at[px * 4 + py], sum_t.at[slot_i], 24, plane_peer(k))
+
+    each(1, 16, part_t)
+    due[24] = sent[24] = sum_t.at[pl.ds(0, 15)]
+    sum_t[slot_i] = par_t[x * 4 + y]
     def last(total, fin, flag, slot, to, sem):
         for k in range(4):
             fin[0, k, 0:20, :] = total[20 * k:20 * k + 20, :]
@@ -347,18 +427,18 @@
         def _():
             drain(fin.at[0], sem)
 
+    arrive(26)
+    last(jnp.sum(sum_i[0:8].astype(F32), axis=0), fin_i, self_i, (y % 2) * 2 + x % 2, to_i, 28)
     arrive(24)
     last(jnp.sum(sum_t[...].astype(F32), axis=0), fin_t, self_t, (z // 4) * 2 + z % 2, to_t, 27)
-    arrive(26)
-    last(jnp.sum(sum_i[0:8].astype(F32), axis=0), fin_i, self_i, (y % 2) * 2 + x % 2, to_i, 28)
 
     def finish(o_ref, fin, flag, sem):
         wait_last(fin, flag, rsem.at[sem])
         for k in range(2):
             o_ref[:, 128 * k:128 * k + 128] = fin[1, k, 0:20, :] + fin[1, 2 + k, 0:20, :]
 
+    finish(oi_ref, fin_i, self_i, 28)
     finish(ot_ref, fin_t, self_t, 27)
-    finish(oi_ref, fin_i, self_i, 28)
 
     for i, ref in sent.items():
         drain(ref, ssem.at[i])
@@ -373,9 +453,10 @@
     return pl.pallas_call(
         kernel,
         out_shape=(out, out),
-        in_specs=[pl.BlockSpec(memory_space=pltpu.SMEM), v, v, v, v],
+        in_specs=[pl.BlockSpec(memory_space=pltpu.SMEM)] + [pl.BlockSpec(memory_space=pl.ANY)] * 4,
         out_specs=(v, v),
         scratch_shapes=[
+            vm((2, 2, 32, 1280), BF16), vm((2, 2, 32, 1280), BF16), vm((1280, 256), BF16), vm((1280, 256), BF16),
             vm((2, 4, 32, 256), F32), vm((2, 4, 32, 256), F32),
             vm((512, 1024), BF16), vm((512, 1024), BF16),
             vm((4, 2, 32, 1280), BF16), vm((2, 4, 32, 1280), BF16),
@@ -383,14 +464,17 @@
             vm((1280, 256), BF16), vm((1280, 256), BF16),
             vm((16, 8, 128), F32), vm((16, 8, 128), F32),
             vm((512, 512), F32), vm((512, 512), F32),
-            vm((2, 8, 128, 256), BF16), vm((2, 8, 128, 256), BF16),
-            vm((8, 128, 256), BF16), vm((2, 4, 128, 256), BF16),
-            vm((16, 128, 256), BF16), vm((8, 128, 256), BF16),
+            vm((4, 4, 2, 64, 256), F32),
+            vm((4, 4, 64, 256), BF16), vm((4, 4, 64, 256), BF16), vm((4, 4, 64, 256), BF16), vm((4, 4, 64, 256), BF16),
+            vm((4, 64, 256), BF16), vm((4, 64, 256), BF16), vm((4, 64, 256), BF16), vm((4, 64, 256), BF16),
+            vm((8, 128, 256), F32), vm((2, 4, 128, 256), BF16), vm((2, 4, 128, 256), BF16),
+            vm((8, 128, 256), BF16), vm((2, 128, 256), BF16), vm((2, 64, 256), BF16), vm((2, 128, 256), BF16),
+            vm((4, 128, 256), BF16),
             vm((16, 80, 128), F32), vm((16, 80, 128), BF16),
             vm((16, 80, 128), BF16), vm((16, 80, 128), BF16),
             vm((8, 80, 128), F32), vm((8, 80, 128), F32),
             vm((2, 4, 24, 128), F32), vm((2, 4, 24, 128), F32),
-            pltpu.SemaphoreType.DMA((32,)), pltpu.SemaphoreType.DMA((32,)),
+            pltpu.SemaphoreType.DMA((34,)), pltpu.SemaphoreType.DMA((34,)), pltpu.SemaphoreType.DMA((4,)),
         ],
         compiler_params=pltpu.CompilerParams(
             collective_id=0, has_side_effects=True, vmem_limit_bytes=56 * 2 ** 20),

time: 73 us -> 67.9 us (0.930)
  Pallas kernels: 69.4 us -> 64.5 us
    pallas_call x1, Pallas kernels: 69.4 us -> 64.5 us  [per_device(): pl.pallas_call(kernel, out_shape=(out, out), in_specs=[pl.BlockSpec(memor...]
where the time goes in v3:
time: 67.9 us; the launch traced here: 67.8 us
  Pallas kernels  64.5 us (95%)
  local copies, waits for them, and re-layouts  1.96 us (3%)
  between operations  1.29 us (2%)
    pallas_call x1, Pallas kernels, per_device(): pl.pallas_call(kernel, out_shape=(out, out), in_specs=[pl.BlockSpec(memor...  64.5 us
    unnamed x4, local copies, waits for them, and re-layouts  1.96 us

profile of v3, /device:TPU:1, one launch (start us, length us, event | category | flops | bytes accessed | tf_op | source)
XLA Modules:
  0.0 67.8 jit_solution(712921166722986396)
XLA Ops:
  1.3 64.5 %contrastive.1 = (f32[20,256]{1,0:T(8,128)}, f32[20,256]{1,0:T(8,128)}) custom-call(f32[1,1]{1,0:T(1,128)} %bitcast.3.scale_ref, bf16[2,2,32,1280]{3,2,1,0:T(8,128)(2,1)} %bitcast.4, bf16[2,2,32,1280]{3,2,1,0:T(8,128)(2,1)} %bitcast.5, bf16[1280,256]{1,0:T(8,128)(2,1)} %wi_ref.1, bf16[1280,256]{1,0:T(8,128)(2,1)} %wt_ref.1), custom_call_target="tpu_custom_call" | custom-call | tf_op jit(solution)/shard_map/contrastive/pallas_call | solution.py:453
  65.8 0.0 copy-start
  65.8 1.4 %copy.10 = f32[20,256]{1,0:T(8,128)} copy(f32[20,256]{1,0:T(8,128)} %get-tuple-element.4) | data formatting | bytes 40960
  67.2 0.0 copy-done
  67.2 0.6 copy.11
Async XLA Ops:
  65.8 1.4 %copy-start = (f32[20,256]{1,0:T(8,128)S(1)}, f32[20,256]{1,0:T(8,128)}, u32[]{:S(2)}) copy-start(f32[20,256]{1,0:T(8,128)} %get-tuple-element.5) | copy-start | bytes 61444

commit v4 on v3

--- a/solution.py
+++ b/solution.py
@@ -41,11 +41,18 @@
     pltpu.make_async_copy(ref, ref, sem).wait()
 
 
-def each(lo, hi, body):
-    def step(k, carry):
+def each(steps, body):
+    for k in steps:
         body(k)
-        return carry
-    lax.fori_loop(lo, hi, step, 0)
+
+
+def hops(k, n):
+    return min(k % n, n - k % n)
+
+
+PLANE = sorted(range(1, 16), key=lambda k: -hops(k, 4) - hops(k // 4, 4))
+LINE = sorted(range(1, 16), key=lambda k: -hops(k, 8))
+COLUMN = [k for k in LINE if k < 8]
 
 
 def to_column(row):
@@ -76,7 +83,7 @@
     return lse, inv
 
 
-def kernel(scale_ref, fi_ref, ft_ref, wi_ref, wt_ref, oi_ref, ot_ref,
+def kernel(scale_ref, fi_ref, ft_ref, wi_ref, wt_ref, o_ref,
            fi_v, ft_v, wi_v, wt_v,
            raw_s, raw_r, emb_i, emb_t, feat_i, feat_t, emb_it, emb_tt, feat_it, feat_tt,
            stat_i, stat_t, log_a, log_b, own_i, dem_x, dem_y, get_x, get_y, dem_x2, dem_y2, last_x, last_y,
@@ -123,12 +130,12 @@
     def hello(peer):
         pl.semaphore_signal(bar, inc=1, device_id=peer, device_id_type=MESH)
 
-    each(1, 4, lambda k: hello(head_peer(k)))
-    each(1, 4, lambda k: hello(device(x + k, y, z, core)))
+    each(range(1, 4), lambda k: hello(head_peer(k)))
+    each(range(1, 4), lambda k: hello(device(x + k, y, z, core)))
     hello(device(x, y + 1, z, core))
     hello(device(x, y - 1, z, core))
-    each(1, 4, lambda k: hello(device(x, y, z + k, core)))
-    each(1, 4, lambda k: hello(device(x, y, z - k, core)))
+    each(range(1, 4), lambda k: hello(device(x, y, z + k, core)))
+    each(range(1, 4), lambda k: hello(device(x, y, z - k, core)))
 
     fetched = [pltpu.make_async_copy(a, b, lsem.at[k])
                for k, (a, b) in enumerate(((fi_ref, fi_v), (wi_ref, wi_v), (ft_ref, ft_v), (wt_ref, wt_v)))]
@@ -147,7 +154,7 @@
         def one(k):
             peer = head_peer(k)
             send(raw_s.at[side, peer["head"]], raw_r.at[side, h], sem, peer)
-        each(1, 4, one)
+        each(range(1, 4), one)
         due[sem] = sent[sem] = raw_s.at[side, pl.ds(0, 3)]
         raw_r[side, h] = raw_s[side, h]
 
@@ -224,21 +231,30 @@
     to_sibling(z + 4)
     due[17] = sent[17] = emb_t.at[pl.ds(0, 256)]
     arrive(11)
+
+    scale = scale_ref[0, 0]
+
+    def logits(part):
+        where = [pl.ds(pl.multiple_of(256 * k + 128 * part, 128), 128) for k in range(2)]
+        texts = jnp.concatenate([emb_t[r, :] for r in where], axis=0)
+        a = scale * lax.dot_general(texts, emb_i[...], NT, preferred_element_type=F32)
+        for k in range(2):
+            log_b[where[k], :] = a[128 * k:128 * k + 128]
+
+    logits(core)
     arrive(17)
-
-    scale = scale_ref[0, 0]
-    log_a[...] = scale * lax.dot_general(emb_i[...], emb_t[...], NT, preferred_element_type=F32)
-    log_b[...] = scale * lax.dot_general(emb_t[...], emb_i[...], NT, preferred_element_type=F32)
+    logits(1 - core)
     put_stats(stat_i.at[slot_i], lse_rows(log_b[...]), inv_i)
+    each(PLANE, lambda k: send(stat_i.at[slot_i], stat_i.at[slot_i], 18, plane_peer(k)))
+    due[18] = sent[18] = stat_i.at[pl.ds(0, 15)]
+    log_a[...] = log_b[...].T
     put_stats(stat_t.at[slot_t], lse_rows(log_a[...]), inv_t)
-    each(1, 16, lambda k: send(stat_i.at[slot_i], stat_i.at[slot_i], 18, plane_peer(k)))
-    due[18] = sent[18] = stat_i.at[pl.ds(0, 15)]
-    each(1, 16, lambda k: send(stat_t.at[slot_t], stat_t.at[slot_t], 19, line_peer(k)))
+    each(LINE, lambda k: send(stat_t.at[slot_t], stat_t.at[slot_t], 19, line_peer(k)))
     due[19] = sent[19] = stat_t.at[pl.ds(0, 15)]
-    each(1, 4, lambda k: send(fi_v.at[:, core], feat_i.at[x], 2, device(x + k, y, z, core)))
+    each(range(1, 4), lambda k: send(fi_v.at[:, core], feat_i.at[x], 2, device(x + k, y, z, core)))
     due[2] = sent[2] = feat_i.at[pl.ds(0, 3)]
     feat_i[x] = fi_v[:, core]
-    each(1, 4, lambda k: send(ft_v.at[y // 2, core], feat_t.at[core, z % 4], 3,
+    each(range(1, 4), lambda k: send(ft_v.at[y // 2, core], feat_t.at[core, z % 4], 3,
                               device(x, y, (z // 4) * 4 + (z + k) % 4, core)))
     due[3] = sent[3] = feat_t.at[0, pl.ds(0, 3)]
     feat_t[core, z % 4] = ft_v[y // 2, core]
@@ -254,32 +270,27 @@
     ids0 = lax.broadcasted_iota(jnp.int32, (512, 512), 0)
     ids1 = lax.broadcasted_iota(jnp.int32, (512, 512), 1)
 
-    def grads(log, along, across, slot0, slot1):
-        a = log[...]
-        same = (ids0 // 32 == slot0) & (ids0 - ids1 == 32 * (slot0 - slot1))
-        g = (jnp.exp(a - along) + jnp.exp(a - across) - jnp.where(same, 2.0, 0.0)) * factor
-        g = g.astype(BF16)
-        return g, jnp.sum(g.astype(F32) * a, axis=0, keepdims=True)
+    a = log_a[...]
+    same = (ids0 // 32 == slot_i) & (ids0 - ids1 == 32 * (slot_i - slot_t))
+    g = (jnp.exp(a - to_column(row_lse)) + jnp.exp(a - col_lse) - jnp.where(same, 2.0, 0.0)) * factor
+    g = g.astype(BF16)
+    inner_t = jnp.sum(g.astype(F32) * a, axis=0, keepdims=True)
 
     def demb(g, inner, base, unit, half):
         part = pl.ds(pl.multiple_of(512 * half, 512), 512)
         d = scale * lax.dot_general(base[part, :], g, NN, preferred_element_type=F32)
         return d - unit[part, :].astype(F32) * inner
 
-    g, inner = grads(log_a, to_column(row_lse), col_lse, slot_i, slot_t)
-    d = demb(g, inner, emb_it, emb_tt, 1 - core)
+    d = demb(g, inner_t, emb_it, emb_tt, 1 - core)
     for k in range(2):
         dem_t[k] = d[:, 256 * k:256 * k + 256].astype(BF16).reshape(4, 128, 256)
     send(dem_t, sib_r, 21, sibling)
     due[21] = sent[21] = sib_r
-    d = demb(g, inner, emb_it, emb_tt, core)
-    for k in range(2):
-        own_t[4 * k:4 * k + 4] = d[:, 256 * k:256 * k + 256].reshape(4, 128, 256)
-
-    g, inner = grads(log_b, row_lse, to_column(col_lse), slot_t, slot_i)
+    gt = g.T
+    inner_i = jnp.sum(gt.astype(F32) * log_b[...], axis=0, keepdims=True)
 
     def image_half(pair):
-        d = demb(g, inner, emb_tt, emb_it, pair)
+        d = demb(gt, inner_i, emb_tt, emb_it, pair)
         for k in range(2):
             py = 2 * pair + k
             e = d[:, 256 * k:256 * k + 256].reshape(4, 2, 64, 256)
@@ -294,10 +305,14 @@
     send_y((y + 2) % 4)
     send_y((1 - y // 2) * 2 + (y + 1) % 2)
     image_half(y // 2)
-    each(0, 3, lambda k: send(dem_x.at[(x + 1 + (k + 1) % 3) % 4], get_x.at[x], 22, device(x + 1 + (k + 1) % 3, y, z, core)))
+    each(range(0, 3), lambda k: send(dem_x.at[(x + 1 + (k + 1) % 3) % 4], get_x.at[x], 22, device(x + 1 + (k + 1) % 3, y, z, core)))
     send_y((y // 2) * 2 + (y + 1) % 2)
     due[22] = sent[22] = get_x.at[pl.ds(0, 3)]
     due[29] = sent[29] = get_y.at[pl.ds(0, 3)]
+    d = demb(g, inner_t, emb_it, emb_tt, core)
+    for k in range(2):
+        own_t[4 * k:4 * k + 4] = d[:, 256 * k:256 * k + 256].reshape(4, 128, 256)
+
     arrive(21)
     own_t[...] = own_t[...] + sib_r[...].astype(F32).reshape(8, 128, 256)
     sib_s[...] = own_t[...].astype(BF16)
@@ -378,6 +393,18 @@
         out_s[k] = par_i[chunk_i(k, 1 - core)]
     send(out_s, out_r, 25, sibling)
     due[25] = sent[25] = out_r
+    arrive(31)
+    total_t = own_t[z] + jnp.sum(get_t[...].astype(F32), axis=0)
+    par_t[...] = weights(total_t, invs_t, z // 4 == 1, feat_tt).astype(BF16)
+
+    def part_t(k):
+        px, py = (x + k % 4) % 4, (y + k // 4) % 4
+        send(par_t.at[px * 4 + py], sum_t.at[slot_i], 24, plane_peer(k))
+
+    each(PLANE, part_t)
+    due[24] = sent[24] = sum_t.at[pl.ds(0, 15)]
+    sum_t[slot_i] = par_t[x * 4 + y]
+
     arrive(25)
     for k in range(8):
         par_t_i = par_i[chunk_i(k, core)] + out_r[k]
@@ -387,22 +414,10 @@
     def part_i(k):
         send(sum_i.at[8 + (z + k) % 8], sum_i.at[z], 26, line_peer(k))
 
-    each(1, 8, part_i)
+    each(COLUMN, part_i)
     due[26] = sent[26] = sum_i.at[pl.ds(0, 7)]
     sum_i[z] = sum_i[8 + z]
 
-
-    arrive(31)
-    total_t = own_t[z] + jnp.sum(get_t[...].astype(F32), axis=0)
-    par_t[...] = weights(total_t, invs_t, z // 4 == 1, feat_tt).astype(BF16)
-
-    def part_t(k):
-        px, py = (x + k % 4) % 4, (y + k // 4) % 4
-        send(par_t.at[px * 4 + py], sum_t.at[slot_i], 24, plane_peer(k))
-
-    each(1, 16, part_t)
-    due[24] = sent[24] = sum_t.at[pl.ds(0, 15)]
-    sum_t[slot_i] = par_t[x * 4 + y]
     def last(total, fin, flag, slot, to, sem):
         for k in range(4):
             fin[0, k, 0:20, :] = total[20 * k:20 * k + 20, :]
@@ -412,7 +427,7 @@
             def _():
                 send(fin.at[0, k], fin.at[1, slot], sem, to(k))
 
-        each(0, 4, one)
+        each(range(0, 4), one)
 
         @pl.when(flag)
         def _():
@@ -437,8 +452,8 @@
         for k in range(2):
             o_ref[:, 128 * k:128 * k + 128] = fin[1, k, 0:20, :] + fin[1, 2 + k, 0:20, :]
 
-    finish(oi_ref, fin_i, self_i, 28)
-    finish(ot_ref, fin_t, self_t, 27)
+    finish(o_ref.at[0], fin_i, self_i, 28)
+    finish(o_ref.at[1], fin_t, self_t, 27)
 
     for i, ref in sent.items():
         drain(ref, ssem.at[i])
@@ -448,13 +463,13 @@
 
 def per_device(feat_img, feat_txt, w_img, w_txt, logit_scale):
     v = pl.BlockSpec(memory_space=pltpu.VMEM)
-    out = jax.ShapeDtypeStruct((20, 256), F32)
+    out = jax.ShapeDtypeStruct((2, 20, 256), F32)
     vm = pltpu.VMEM
-    return pl.pallas_call(
+    o = pl.pallas_call(
         kernel,
-        out_shape=(out, out),
+        out_shape=out,
         in_specs=[pl.BlockSpec(memory_space=pltpu.SMEM)] + [pl.BlockSpec(memory_space=pl.ANY)] * 4,
-        out_specs=(v, v),
+        out_specs=v,
         scratch_shapes=[
             vm((2, 2, 32, 1280), BF16), vm((2, 2, 32, 1280), BF16), vm((1280, 256), BF16), vm((1280, 256), BF16),
             vm((2, 4, 32, 256), F32), vm((2, 4, 32, 256), F32),
@@ -480,6 +495,7 @@
             collective_id=0, has_side_effects=True, vmem_limit_bytes=56 * 2 ** 20),
         name="contrastive",
     )(logit_scale.reshape(1, 1), feat_img.reshape(2, 2, 32, 1280), feat_txt.reshape(2, 2, 32, 1280), w_img, w_txt)
+    return o[0], o[1]
 
 
 def solution(mesh):

time: 67.9 us -> 66 us (0.972)
  Pallas kernels: 64.5 us -> 63.2 us
    unnamed x4 -> x0, local copies, waits for them, and re-layouts: 1.96 us -> none
    squeeze x0 -> x1, local copies, waits for them, and re-layouts: none -> 1.38 us  [per_device(): return (o[0], o[1])]
    pallas_call x1, Pallas kernels: 64.5 us -> 63.2 us  [per_device(): pl.pallas_call(kernel, out_shape=out, in_specs=[pl.BlockSpec(memory_space...]
where the time goes in v4:
time: 66 us; the launch traced here: 65.9 us
  Pallas kernels  63.2 us (96%)
  local copies, waits for them, and re-layouts  1.38 us (2%)
  between operations  1.29 us (2%)
    pallas_call x1, Pallas kernels, per_device(): pl.pallas_call(kernel, out_shape=out, in_specs=[pl.BlockSpec(memory_space...  63.2 us
    squeeze x1, local copies, waits for them, and re-layouts, per_device(): return (o[0], o[1])  1.38 us

profile of v4, /device:TPU:1, one launch (start us, length us, event | category | flops | bytes accessed | tf_op | source)
XLA Modules:
  0.0 65.9 jit_solution(12499218927567226224)
XLA Ops:
  1.3 63.2 %contrastive.1 = f32[2,20,256]{2,1,0:T(8,128)} custom-call(f32[1,1]{1,0:T(1,128)} %bitcast.7.scale_ref, bf16[2,2,32,1280]{3,2,1,0:T(8,128)(2,1)} %bitcast.8, bf16[2,2,32,1280]{3,2,1,0:T(8,128)(2,1)} %bitcast.9, bf16[1280,256]{1,0:T(8,128)(2,1)} %wi_ref.1, bf16[1280,256]{1,0:T(8,128)(2,1)} %wt_ref.1), custom_call_target="tpu_custom_call" | custom-call | tf_op jit(solution)/shard_map/contrastive/pallas_call | solution.py:468
  64.5 1.4 %slice_bitcast_fusion = (f32[20,256]{1,0:T(8,128)}, f32[20,256]{1,0:T(8,128)}) fusion(f32[2,20,256]{2,1,0:T(8,128)} %contrastive.1), kind=kLoop, calls=%fused_computation | loop fusion | bytes 81920 | tf_op jit(solution)/shard_map/squeeze | solution.py:498

commit v5 on v4

--- a/solution.py
+++ b/solution.py
@@ -88,7 +88,7 @@
            raw_s, raw_r, emb_i, emb_t, feat_i, feat_t, emb_it, emb_tt, feat_it, feat_tt,
            stat_i, stat_t, log_a, log_b, own_i, dem_x, dem_y, get_x, get_y, dem_x2, dem_y2, last_x, last_y,
            own_t, dem_t, sib_r, sib_s, full_z, half_z, sum_z, get_t,
-           par_i, par_t, sum_i, sum_t, out_s, out_r, fin_i, fin_t, ssem, rsem, lsem):
+           par_i, par_t, line_s, sum_i, sum_t, out_s, out_r, fin_i, fin_t, ssem, rsem, lsem):
     x, y, z, core = place()
     h = lax.axis_index("head")
     slot_i = image_slot(x, y)
@@ -116,14 +116,19 @@
         return device(x, y, z + k % 8, (core + k // 8) % 2)
 
     self_i = (z % 2 == x // 2) & (core == x % 2) & (core == x // 2)
-    self_t = (y == z // 2) & (core == y // 2) & ((z % 4) // 2 == core)
     quarter = (z % 2) * 2 + y % 2
 
     def to_i(e):
         return device((z % 2) * 2 + core, (y // 2) * 2 + e % 2, (z // 2) * 2 + e // 2, x // 2)
 
+    def text_pair(py):
+        step = 1 - 2 * (z % 2)
+        inside = jnp.where(py % 2 == 0, 2, step)
+        outside = jnp.where(py % 2 == 0, -step, 0)
+        return (z // 2 + jnp.where(py // 2 == core, inside, outside) + 4) % 4
+
     def to_t(e):
-        return device(x, core * 2 + e % 2, 2 * y + e // 2, (z % 4) // 2)
+        return device(x, core * 2 + e % 2, 2 * text_pair(y) + e // 2, (z % 4) // 2)
 
     bar = pltpu.get_barrier_semaphore()
 
@@ -363,15 +368,16 @@
         send(sum_z.at[k], get_t.at[2 + k], 31, device(x, y, z + 2 * s, core))
     due[31] = sent[31] = get_t
 
-    def weights(total, invs, upper, feats):
-        inv = jnp.where(upper, invs[:, 256:512], invs[:, 0:256])
-        draw = inv * total
+    def split(total, invs, upper):
+        draw = jnp.where(upper, invs[:, 256:512], invs[:, 0:256]) * total
         high = draw.astype(BF16)
-        low = (draw - high.astype(F32)).astype(BF16)
-        f = feats[...]
+        return high, (draw - high.astype(F32)).astype(BF16)
+
+    def weights(f, draw):
+        high, low = draw
         out = lax.dot_general(f, high, NT, preferred_element_type=F32)
         out += lax.dot_general(f, low, NT, preferred_element_type=F32)
-        return out.reshape(16, 80, 128)
+        return out.reshape(-1, 80, 128)
 
     def image_sum(own, first, lines, last, at):
         total = own
@@ -382,58 +388,65 @@
 
     arrive(32)
     arrive(33)
-    def chunk_i(pz, pc):
-        return ((pz % 2) * 2 + pc) * 4 + pz // 2
-
     upper_cols = image_sum(own_i[y, x, 0], lambda j: get_x[j, y], y, last_x, x)
     lower_cols = image_sum(own_i[y, x, 1], lambda j: get_y[j, x], x, last_y, y)
     total_i = jnp.concatenate([upper_cols, lower_cols], axis=0)
-    par_i[...] = weights(total_i, invs_i, y % 2 == 1, feat_it)
-    for k in range(8):
-        out_s[k] = par_i[chunk_i(k, 1 - core)]
+    draw_i = split(total_i, invs_i, y % 2 == 1)
+
+    def image_rows(k, owner):
+        return weights(feat_it[pl.ds(pl.multiple_of(640 * k + 320 * owner, 320), 320), :], draw_i)
+
+    for k in range(2):
+        out_s[k] = image_rows(k, 1 - core)
     send(out_s, out_r, 25, sibling)
     due[25] = sent[25] = out_r
+    for k in range(2):
+        par_i[k] = image_rows(k, core)
+
     arrive(31)
     total_t = own_t[z] + jnp.sum(get_t[...].astype(F32), axis=0)
-    par_t[...] = weights(total_t, invs_t, z // 4 == 1, feat_tt).astype(BF16)
+    par_t[...] = weights(feat_tt[...], split(total_t, invs_t, z // 4 == 1)).astype(BF16)
 
     def part_t(k):
         px, py = (x + k % 4) % 4, (y + k // 4) % 4
-        send(par_t.at[px * 4 + py], sum_t.at[slot_i], 24, plane_peer(k))
+        send(par_t.at[px * 4 + text_pair(py)], sum_t.at[slot_i], 24, plane_peer(k))
 
     each(PLANE, part_t)
     due[24] = sent[24] = sum_t.at[pl.ds(0, 15)]
-    sum_t[slot_i] = par_t[x * 4 + y]
+    sum_t[slot_i] = par_t[x * 4 + text_pair(y)]
 
     arrive(25)
-    for k in range(8):
-        par_t_i = par_i[chunk_i(k, core)] + out_r[k]
-        sib_p = par_t_i.astype(BF16)
-        sum_i[8 + k] = sib_p
+    line_s[...] = (par_i[...] + out_r[...]).astype(BF16)
 
     def part_i(k):
-        send(sum_i.at[8 + (z + k) % 8], sum_i.at[z], 26, line_peer(k))
+        pz = (z + k) % 8
+        send(line_s.at[pz % 2, pz // 2], sum_i.at[z], 26, line_peer(k))
 
     each(COLUMN, part_i)
     due[26] = sent[26] = sum_i.at[pl.ds(0, 7)]
-    sum_i[z] = sum_i[8 + z]
+    sum_i[z] = line_s[z % 2, z // 2]
 
     def last(total, fin, flag, slot, to, sem):
         for k in range(4):
             fin[0, k, 0:20, :] = total[20 * k:20 * k + 20, :]
-
-        def one(k):
+            if flag is None:
+                send(fin.at[0, k], fin.at[1, slot], sem, to(k))
+                continue
+
             @pl.when(jnp.logical_not(flag & (k == quarter)))
             def _():
                 send(fin.at[0, k], fin.at[1, slot], sem, to(k))
 
-        each(range(0, 4), one)
-
-        @pl.when(flag)
-        def _():
-            fin[1, slot] = fin[0, quarter]
+        if flag is not None:
+            @pl.when(flag)
+            def _():
+                fin[1, slot] = fin[0, quarter]
 
     def wait_last(fin, flag, sem):
+        if flag is None:
+            drain(fin.at[0], sem)
+            return
+
         @pl.when(flag)
         def _():
             drain(fin.at[0, pl.ds(0, 3)], sem)
@@ -442,10 +455,10 @@
         def _():
             drain(fin.at[0], sem)
 
+    arrive(24)
+    last(jnp.sum(sum_t[...].astype(F32), axis=0), fin_t, None, (z // 4) * 2 + z % 2, to_t, 27)
     arrive(26)
-    last(jnp.sum(sum_i[0:8].astype(F32), axis=0), fin_i, self_i, (y % 2) * 2 + x % 2, to_i, 28)
-    arrive(24)
-    last(jnp.sum(sum_t[...].astype(F32), axis=0), fin_t, self_t, (z // 4) * 2 + z % 2, to_t, 27)
+    last(jnp.sum(sum_i[...].astype(F32), axis=0), fin_i, self_i, (y % 2) * 2 + x % 2, to_i, 28)
 
     def finish(o_ref, fin, flag, sem):
         wait_last(fin, flag, rsem.at[sem])
@@ -453,11 +466,11 @@
             o_ref[:, 128 * k:128 * k + 128] = fin[1, k, 0:20, :] + fin[1, 2 + k, 0:20, :]
 
     finish(o_ref.at[0], fin_i, self_i, 28)
-    finish(o_ref.at[1], fin_t, self_t, 27)
+    finish(o_ref.at[1], fin_t, None, 27)
 
     for i, ref in sent.items():
         drain(ref, ssem.at[i])
-    wait_last(fin_t, self_t, ssem.at[27])
+    wait_last(fin_t, None, ssem.at[27])
     wait_last(fin_i, self_i, ssem.at[28])
 
 
@@ -485,9 +498,9 @@
             vm((8, 128, 256), F32), vm((2, 4, 128, 256), BF16), vm((2, 4, 128, 256), BF16),
             vm((8, 128, 256), BF16), vm((2, 128, 256), BF16), vm((2, 64, 256), BF16), vm((2, 128, 256), BF16),
             vm((4, 128, 256), BF16),
-            vm((16, 80, 128), F32), vm((16, 80, 128), BF16),
-            vm((16, 80, 128), BF16), vm((16, 80, 128), BF16),
-            vm((8, 80, 128), F32), vm((8, 80, 128), F32),
+            vm((2, 4, 80, 128), F32), vm((16, 80, 128), BF16), vm((2, 4, 80, 128), BF16),
+            vm((8, 80, 128), BF16), vm((16, 80, 128), BF16),
+            vm((2, 4, 80, 128), F32), vm((2, 4, 80, 128), F32),
             vm((2, 4, 24, 128), F32), vm((2, 4, 24, 128), F32),
             pltpu.SemaphoreType.DMA((34,)), pltpu.SemaphoreType.DMA((34,)), pltpu.SemaphoreType.DMA((4,)),
         ],

time: 66 us -> 64 us (0.970)
  Pallas kernels: 63.2 us -> 61.1 us
    pallas_call x1, Pallas kernels: 63.2 us -> 61.1 us  [per_device(): pl.pallas_call(kernel, out_shape=out, in_specs=[pl.BlockSpec(memory_space...]
where the time goes in v5:
time: 64 us; the launch traced here: 63.8 us
  Pallas kernels  61.1 us (95%)
  local copies, waits for them, and re-layouts  1.38 us (2%)
  between operations  1.29 us (2%)
    pallas_call x1, Pallas kernels, per_device(): pl.pallas_call(kernel, out_shape=out, in_specs=[pl.BlockSpec(memory_space...  61.1 us
    squeeze x1, local copies, waits for them, and re-layouts, per_device(): return (o[0], o[1])  1.38 us

profile of v5, /device:TPU:1, one launch (start us, length us, event | category | flops | bytes accessed | tf_op | source)
XLA Modules:
  0.0 63.8 jit_solution(3392238803869219715)
XLA Ops:
  1.3 61.1 %contrastive.1 = f32[2,20,256]{2,1,0:T(8,128)} custom-call(f32[1,1]{1,0:T(1,128)} %bitcast.7.scale_ref, bf16[2,2,32,1280]{3,2,1,0:T(8,128)(2,1)} %bitcast.8, bf16[2,2,32,1280]{3,2,1,0:T(8,128)(2,1)} %bitcast.9, bf16[1280,256]{1,0:T(8,128)(2,1)} %wi_ref.1, bf16[1280,256]{1,0:T(8,128)(2,1)} %wt_ref.1), custom_call_target="tpu_custom_call" | custom-call | tf_op jit(solution)/shard_map/contrastive/pallas_call | solution.py:481
  62.4 1.4 %slice_bitcast_fusion = (f32[20,256]{1,0:T(8,128)}, f32[20,256]{1,0:T(8,128)}) fusion(f32[2,20,256]{2,1,0:T(8,128)} %contrastive.1), kind=kLoop, calls=%fused_computation | loop fusion | bytes 81920 | tf_op jit(solution)/shard_map/squeeze | solution.py:511

commit v6 on v5

--- a/solution.py
+++ b/solution.py
@@ -289,7 +289,7 @@
     d = demb(g, inner_t, emb_it, emb_tt, 1 - core)
     for k in range(2):
         dem_t[k] = d[:, 256 * k:256 * k + 256].astype(BF16).reshape(4, 128, 256)
-    send(dem_t, sib_r, 21, sibling)
+        send(dem_t.at[k], sib_r.at[k], 21, sibling)
     due[21] = sent[21] = sib_r
     gt = g.T
     inner_i = jnp.sum(gt.astype(F32) * log_b[...], axis=0, keepdims=True)
@@ -398,7 +398,7 @@
 
     for k in range(2):
         out_s[k] = image_rows(k, 1 - core)
-    send(out_s, out_r, 25, sibling)
+        send(out_s.at[k], out_r.at[k], 25, sibling)
     due[25] = sent[25] = out_r
     for k in range(2):
         par_i[k] = image_rows(k, core)

time: 64 us -> 64 us (level)
  no operation moved by 1% of the time
where the time goes in v6:
time: 64 us; the launch traced here: 63.8 us
  Pallas kernels  61.1 us (95%)
  local copies, waits for them, and re-layouts  1.38 us (2%)
  between operations  1.29 us (2%)
    pallas_call x1, Pallas kernels, per_device(): pl.pallas_call(kernel, out_shape=out, in_specs=[pl.BlockSpec(memory_space...  61.1 us
    squeeze x1, local copies, waits for them, and re-layouts, per_device(): return (o[0], o[1])  1.38 us

profile of v6, /device:TPU:1, one launch (start us, length us, event | category | flops | bytes accessed | tf_op | source)
XLA Modules:
  0.0 63.8 jit_solution(7575851688870682391)
XLA Ops:
  1.3 61.1 %contrastive.1 = f32[2,20,256]{2,1,0:T(8,128)} custom-call(f32[1,1]{1,0:T(1,128)} %bitcast.7.scale_ref, bf16[2,2,32,1280]{3,2,1,0:T(8,128)(2,1)} %bitcast.8, bf16[2,2,32,1280]{3,2,1,0:T(8,128)(2,1)} %bitcast.9, bf16[1280,256]{1,0:T(8,128)(2,1)} %wi_ref.1, bf16[1280,256]{1,0:T(8,128)(2,1)} %wt_ref.1), custom_call_target="tpu_custom_call" | custom-call | tf_op jit(solution)/shard_map/contrastive/pallas_call | solution.py:481
  62.4 1.4 %slice_bitcast_fusion = (f32[20,256]{1,0:T(8,128)}, f32[20,256]{1,0:T(8,128)}) fusion(f32[2,20,256]{2,1,0:T(8,128)} %contrastive.1), kind=kLoop, calls=%fused_computation | loop fusion | bytes 81920 | tf_op jit(solution)/shard_map/squeeze | solution.py:511
